TPU v7x, 512 devices: a whole 4x8x8 slice. The times are simulated.
512 devices in a mesh: row: 32 (over x, y), col: 16 (over z, core).
Axes of the slice: x: 4, y: 8, z: 8, core: 2. Of those that a mesh axis runs over, the one named last changes fastest.
Arguments:
- momentum: float32 [8192, 13312], P('row', 'col'), may hold values from -200 to 200
- gradient: bfloat16 [8192, 13312], P('row', 'col'), may hold values from -6 to 6
- basis: float32 [13312, 256], P('col'), may hold values from -0.0546875 to 0.0546875
Outputs:
- new_momentum: float32 [8192, 13312], P('row', 'col')
- new_basis: float32 [13312, 256], P('col')
- update: bfloat16 [8192, 13312], P('row', 'col')
All inputs are finite; a program needn't handle non-finite values.
Results may differ from a plain program's by a relative error of at most 0.001.
Values sent between devices are 32-bit elements; how exact they have to be, the bound alone decides.
A program may use at most 64 MiB of HBM per device.

v0:
```python
import math

import jax
import jax.numpy as jnp
from jax import lax
from jax.sharding import PartitionSpec as P

M = 8192
N = 13312
R = 256


KEEP_RATE = 0.95
NORM_EPS = 1e-06


def shards(momentum, gradient, basis):
    high = lax.Precision.HIGHEST
    buffer = momentum + gradient.astype(jnp.float32)
    partial_power = jnp.dot(buffer, basis, precision=high, preferred_element_type=jnp.float32)
    power = lax.psum(partial_power, "col")
    local_gram = lax.dot_general(
        power, power, (((0,), (0,)), ((), ())), precision=high, preferred_element_type=jnp.float32
    )
    gram = lax.psum(local_gram, "row")
    lower = jnp.linalg.cholesky(gram)
    ortho = lax.linalg.triangular_solve(lower, power, left_side=False, lower=True, transpose_a=True)
    local_right = lax.dot_general(
        buffer, ortho, (((0,), (0,)), ((), ())), precision=high, preferred_element_type=jnp.float32
    )
    right = lax.psum(local_right, "row")
    squares = lax.psum(jnp.sum(right * right, axis=0), "col")
    norms = jnp.sqrt(squares) + NORM_EPS
    new_basis = right / norms[None, :]
    feedback = lax.dot_general(
        ortho, right, (((1,), (1,)), ((), ())), precision=high, preferred_element_type=jnp.float32
    )
    new_momentum = buffer - (1.0 - KEEP_RATE) * feedback
    factor = math.sqrt(M * N / R)
    product = lax.dot_general(
        ortho,
        new_basis,
        (((1,), (1,)), ((), ())),
        precision=high,
        preferred_element_type=jnp.float32,
    )
    update = (factor * product).astype(jnp.bfloat16)
    return (new_momentum, new_basis, update)


def solution(mesh):
    return jax.shard_map(
        shards,
        mesh=mesh,
        in_specs=(P("row", "col"), P("row", "col"), P("col", None)),
        out_specs=(P("row", "col"), P("col", None), P("row", "col")),
        check_vma=False,
    )
```

profile of v0, /device:TPU:1, one launch (start us, length us, event | category | flops | bytes accessed | tf_op | source)
XLA Modules:
  0.0 548.0 jit_solution(7173095394573096627)
XLA Ops:
  7.2 1.1 copy-done
  8.3 3.6 fusion.3
  11.9 0.0 all-reduce.7.cloned.1.call-start
  12.0 120.4 %all-reduce.5.cloned.1.call-done = f32[256,256]{1,0:T(8,128)} async-done(((f32[256,256]{1,0:T(8,128)}), f32[256,256]{1,0:T(8,128)}) %all-reduce.5.cloned.1.call-update) | async-done | bytes 262160 | tf_op jit(solution)/shard_map/psum | solution.py:21
  132.4 2.3 fusion.16
  134.7 0.2 all-reduce.9.cloned.1.call-start
  135.0 152.3 %all-reduce.7.cloned.1.call-done = f32[256,256]{0,1:T(8,128)} async-done(((f32[256,256]{0,1:T(8,128)}), f32[256,256]{0,1:T(8,128)}) %all-reduce.7.cloned.1.call-update) | async-done | bytes 262160 | tf_op jit(solution)/shard_map/psum | solution.py:25
  287.3 1.1 copy.7
  288.5 11.7 %cholesky.50 = f32[128,128]{1,0:T(8,128)S(1)} custom-call(f32[128,128]{1,0:T(8,128)S(1)} %cholesky.118), custom_call_target="Cholesky" | custom-call | tf_op jit(solution)/shard_map/jit(cholesky)/cholesky | solution.py:26
  300.3 9.8 %custom-call.14 = f32[1,128,128]{1,2,0:T(8,128)S(1)} custom-call(f32[1,128,128]{2,1,0:T(8,128)S(1)} %get-tuple-element.24), custom_call_target="InvertDiagBlocksLowerTriangular" | custom-call | tf_op jit(solution)/shard_map/jit(cholesky)/cholesky | solution.py:26
  310.1 0.2 constant_dynamic-update-slice_fusion.1
  310.3 0.3 convolution_subtract_fusion.1
  310.6 11.7 %cholesky.105 = f32[128,128]{1,0:T(8,128)S(1)} custom-call(f32[128,128]{1,0:T(8,128)S(1)} %convolution_subtract_fusion.1), custom_call_target="Cholesky" | custom-call | tf_op jit(solution)/shard_map/jit(cholesky)/cholesky | solution.py:26
  322.3 0.6 compare_reduce_fusion
  324.3 0.1 triangular_solve.58
  324.4 4.2 while.1
  324.6 0.6 fusion.27
  325.2 1.4 bitcast_dynamic-update-slice_fusion.2
  326.6 0.6 fusion.27
  327.2 1.4 bitcast_dynamic-update-slice_fusion.2
  328.6 19.7 %custom-call.15 = f32[2,128,128]{1,2,0:T(8,128)S(1)} custom-call(f32[2,128,128]{2,1,0:T(8,128)S(1)} %get-tuple-element.10), custom_call_target="InvertDiagBlocksLowerTriangular" | custom-call | tf_op jit(solution)/shard_map/triangular_solve | solution.py:27
  348.3 0.3 fusion.5
  348.6 0.4 convolution_subtract_fusion
  349.0 0.3 fusion.7
  349.3 0.3 copy-done.3
  349.6 1.8 fusion.2
  351.4 155.9 %all-reduce.9.cloned.1.call-done = f32[832,256]{1,0:T(8,128)} async-done(((f32[832,256]{1,0:T(8,128)}), f32[832,256]{1,0:T(8,128)}) %all-reduce.9.cloned.1.call-update) | async-done | bytes 851984 | tf_op jit(solution)/shard_map/psum | solution.py:31
  507.3 1.4 multiply_reduce_fusion
  508.6 29.4 %psum.31 = f32[256]{0:T(256)S(1)} all-reduce(f32[256]{0:T(256)S(1)} %multiply_reduce_fusion), channel_id=1, replica_groups=mesh['row'=32,'col'=16] {'col'}, use_global_device_ids=true, to_apply=%region_8.9 | all-reduce | flops 256 | bytes 2048 | tf_op jit(solution)/shard_map/psum | solution.py:32
  538.0 0.1 broadcast_divide_fusion
  538.1 1.6 fusion.1
  539.7 1.8 fusion
  (27 shorter events, 0.3 us)
Async XLA Ops:
  7.2 1.2 copy-start
  7.2 125.2 %all-reduce.5.cloned.1.call-start = ((), (), s32[]{:S(2)}) async-start(), calls=%async_computation | async-start | bytes 524288 | tf_op jit(solution)/shard_map/psum | solution.py:21
  11.9 275.3 %all-reduce.7.cloned.1.call-start = ((), (), s32[]{:S(2)}) async-start(), calls=%async_computation.1 | async-start | bytes 524288 | tf_op jit(solution)/shard_map/psum | solution.py:25
  134.7 372.5 %all-reduce.9.cloned.1.call-start = ((), (), s32[]{:S(2)}) async-start(), calls=%async_computation.2 | async-start | bytes 1703936 | tf_op jit(solution)/shard_map/psum | solution.py:31
  287.3 1.2 copy-start.6
  324.3 24.0 %copy-start.5 = (f32[256,256]{1,0:T(8,128)S(1)}, f32[256,256]{1,0:T(8,128)}, u32[]{:S(2)}) copy-start(f32[256,256]{1,0:T(8,128)} %all-reduce.5.cloned.1.call-done) | copy-start | bytes 786436
  324.4 24.9 %copy-start.2 = (f32[256,832]{0,1:T(8,128)S(1)}, f32[256,832]{0,1:T(8,128)}, u32[]{:S(2)}) copy-start(f32[256,832]{0,1:T(8,128)} %param.3) | copy-start | bytes 2555908
  348.6 1.0 copy-start.3
  507.3 30.7 %copy-start.1 = (f32[832,256]{1,0:T(8,128)S(1)}, f32[832,256]{1,0:T(8,128)}, u32[]{:S(2)}) copy-start(f32[832,256]{1,0:T(8,128)} %all-reduce.9.cloned.1.call-done) | copy-start | bytes 2555908
  538.1 3.4 copy-start.4
Sparse Core Ops, SparseCore 0:
  12.1 120.2 all-reduce.4
  136.8 150.4 all-reduce.6
  351.5 155.6 all-reduce.8
where the time goes:
time: 548 us
  waiting for transfers between devices  429 us (78%)
  other arithmetic  55.1 us (10%)
  blocking collectives  29.4 us (5%)
  between operations  15.2 us (3%)
  matrix products  12.6 us (2%)
  local copies, waits for them, and re-layouts  6.6 us (1%)
    psum x1, waiting for transfers between devices, shards(): right = lax.psum(local_right, 'row')  156 us
    psum x1, waiting for transfers between devices, shards(): gram = lax.psum(local_gram, 'row')  152 us
    psum x1, waiting for transfers between devices, shards(): power = lax.psum(partial_power, 'col')  120 us
    another operation x6, other arithmetic, shards(): lower = jnp.linalg.cholesky(gram)  34 us
    psum x1, blocking collectives, shards(): squares = lax.psum(jnp.sum(right * right, axis=0), 'col')  29.4 us
    another operation x3, other arithmetic, shards(): lax.linalg.triangular_solve(lower, power, left_side=False, lower=True, tr...  19.7 us
  transfers between devices with their start and end apart: 3, of which 3 were waited for; matrix products, arithmetic and copies ran while one was open for 0% of the time, Pallas kernels for 0%

commit v1 on v0

v1 whole, which is shorter than its diff:
```python
import functools
import math

import jax
import jax.numpy as jnp
from jax import lax
from jax.experimental import pallas as pl
from jax.experimental.pallas import tpu as pltpu
from jax.sharding import PartitionSpec as P

M = 8192
N = 13312
R = 256
KEEP_RATE = 0.95
NORM_EPS = 1e-06

NX, NY, NZ = 4, 8, 8
ROWS = M // (NX * NY)
COLS = N // (2 * NZ)
WIDE = 896
CUT = 512
REST = WIDE - CUT
F32 = jnp.float32
BF16 = jnp.bfloat16
MESH = pl.DeviceIdType.MESH


def dot(a, b, dims):
    return lax.dot_general(
        a, b, (dims, ((), ())), precision=lax.Precision.HIGHEST, preferred_element_type=F32
    )


def factor_step(k, a, rs):
    off = pl.multiple_of(k * 8, 8)
    diag = pltpu.roll(a[pl.ds(off, 8), :R], lax.rem(R - off, R), 1)[:, :128]
    s = {}
    for j in range(8):
        col = jnp.broadcast_to(diag[:, j : j + 1], (8, 128))
        for i in range(j, 8):
            s[i, j] = jnp.broadcast_to(col[i : i + 1, :], (8, 128))
    rows = [a[pl.ds(off + i, 1), :] for i in range(8)]
    for j in range(8):
        d = lax.rsqrt(s[j, j])
        rows[j] = rows[j] * jnp.concatenate([d[:1]] * 4, axis=1)
        rs[j : j + 1, :] = rows[j]
        l = {i: s[i, j] * d for i in range(j + 1, 8)}
        for i in range(j + 1, 8):
            rows[i] = rows[i] - jnp.concatenate([l[i][:1]] * 4, axis=1) * rows[j]
            for c in range(j + 1, i + 1):
                s[i, c] = s[i, c] - l[i] * l[c]
    r = rs[...]
    a[pl.ds(off, 8), R:] = r[:, R:]
    hi = r.astype(BF16).astype(F32)
    mi = (r - hi).astype(BF16).astype(F32)
    lo = r - hi - mi
    lane = lax.broadcasted_iota(jnp.int32, (48, R), 1)
    lhs = jnp.concatenate([hi, hi, mi, mi, hi, lo], axis=0)[:, :R]
    lhs = jnp.where(lane >= off + 8, lhs, 0.0).astype(BF16)
    rhs = jnp.concatenate([hi, mi, hi, mi, lo, hi], axis=0).astype(BF16)
    a[...] = a[...] - lax.dot_general(
        lhs, rhs, (((0,), (0,)), ((), ())), preferred_element_type=F32
    )


def kernel(
    mom_ref, grad_ref, basis_ref,
    nm_ref, nb_ref, up_ref,
    buf, part, core_in, half, z_in, power,
    gram, gx, gy, gram_all,
    wt1, wt2, wx1_in, sx1, wy1_in, wy2_in, sy2, wx2_in, wf1, wf2,
    a, rs, right, sq,
    s_core, r_core, s_zr, r_zr, s_zg, r_zg, s_cg, r_cg,
    s_gx, r_gx, s_gy, r_gy, s_gz, r_gz, s_gc, r_gc,
    s_x1, r_x1, s_y1, r_y1, s_y2, r_y2, s_x2, r_x2,
    s_y1g, r_y1g, s_x1g, r_x1g, s_x2g, r_x2g, s_y2g, r_y2g,
    s_sq, r_sq,
):
    row = lax.axis_index("row")
    col = lax.axis_index("col")
    x, y = row // NY, lax.rem(row, NY)
    z, core = col // 2, lax.rem(col, 2)

    def x_peer(k):
        xt = lax.rem(x + k, NX)
        return xt, (xt * NY + y, col)

    def y_peer(k):
        yt = lax.rem(y + k, NY)
        return yt, (x * NY + yt, col)

    def z_peer(k):
        zt = lax.rem(z + k, NZ)
        return zt, (row, zt * 2 + core)

    sibling = (row, z * 2 + 1 - core)

    def col_peer(k):
        return (row, lax.rem(col + k, 2 * NZ))

    sent = []

    def send(src, dst, ssem, rsem, dev):
        copy = pltpu.make_async_remote_copy(
            src_ref=src, dst_ref=dst, send_sem=ssem, recv_sem=rsem,
            device_id=dev, device_id_type=MESH,
        )
        copy.start()
        sent.append(copy)
        return copy

    def rows8(start, n):
        return pl.ds(pl.multiple_of(start, 8), n)

    barrier = pltpu.get_barrier_semaphore()
    peers = [x_peer(k)[1] for k in range(1, NX)]
    peers += [y_peer(k)[1] for k in range(1, NY)]
    peers += [col_peer(k) for k in range(1, 2 * NZ)]
    for dev in peers:
        pl.semaphore_signal(barrier, inc=1, device_id=dev, device_id_type=MESH)

    buf[:, COLS:] = jnp.zeros((ROWS, WIDE - COLS), F32)
    buf[:, :COLS] = mom_ref[...] + grad_ref[...].astype(F32)
    part[...] = dot(buf[:, :COLS], basis_ref[...], ((1,), (0,)))

    pl.semaphore_wait(barrier, len(peers))

    c = send(part.at[rows8((1 - core) * 128, 128), :], core_in, s_core, r_core, sibling)
    c.wait_recv()
    half[...] = part[rows8(core * 128, 128), :] + core_in[...]
    cs = []
    for k in range(1, NZ):
        zt, dev = z_peer(k)
        cs.append(send(half.at[rows8(zt * 16, 16), :], z_in.at[k - 1], s_zr.at[k - 1], r_zr.at[k - 1], dev))
    total = half[rows8(z * 16, 16), :]
    for k in range(1, NZ):
        cs[k - 1].wait_recv()
        total = total + z_in[k - 1]

    def gather_col(ref, ss, rr, sc, rc):
        mine = ref.at[rows8(core * 128 + z * 16, 16), :]
        cs = []
        for k in range(1, NZ):
            cs.append(send(mine, mine, ss.at[k - 1], rr.at[k - 1], z_peer(k)[1]))
        fs = [send(mine, mine, sc.at[0], rc.at[0], sibling)]
        for k in range(1, NZ):
            cs[k - 1].wait_recv()
            zs = lax.rem(z + NZ - k, NZ)
            theirs = ref.at[rows8(core * 128 + zs * 16, 16), :]
            fs.append(send(theirs, theirs, sc.at[k], rc.at[k], sibling))
        return fs

    power[rows8(core * 128 + z * 16, 16), :] = total
    for c in gather_col(power, s_zg, r_zg, s_cg, r_cg):
        c.wait_recv()

    gram[...] = dot(power[...], power[...], ((0,), (0,)))
    gs = rows8(core * 128 + z * 16, 16)
    cs = []
    for k in range(1, NX):
        cs.append(send(gram.at[gs, :], gx.at[x], s_gx.at[k - 1], r_gx.at[k - 1], x_peer(k)[1]))
    gx[x] = gram[gs, :]

    wt1[...] = dot(power[...], buf[:, :CUT], ((0,), (0,)))
    c_x1 = []
    for k in range(1, NX):
        xt, dev = x_peer(k)
        c_x1.append(send(wt1.at[rows8(xt * 64, 64), :], wx1_in.at[k - 1], s_x1.at[k - 1], r_x1.at[k - 1], dev))

    for c in cs:
        c.wait_recv()
    gy[y] = (gx[0] + gx[1]) + (gx[2] + gx[3])
    cs = []
    for k in range(1, NY):
        cs.append(send(gy.at[y], gy.at[y], s_gy.at[k - 1], r_gy.at[k - 1], y_peer(k)[1]))

    wt2[...] = dot(power[...], buf[:, CUT:], ((0,), (0,)))
    c_y2 = []
    for k in range(1, NY):
        yt, dev = y_peer(k)
        c_y2.append(send(wt2.at[rows8(yt * 32, 32), :], wy2_in.at[k - 1], s_y2.at[k - 1], r_y2.at[k - 1], dev))

    for c in cs:
        c.wait_recv()
    gram_all[gs, :] = ((gy[0] + gy[1]) + (gy[2] + gy[3])) + ((gy[4] + gy[5]) + (gy[6] + gy[7]))
    fs = gather_col(gram_all, s_gz, r_gz, s_gc, r_gc)

    for c in c_x1:
        c.wait_recv()
    sx1[...] = (wt1[rows8(x * 64, 64), :] + wx1_in[0]) + (wx1_in[1] + wx1_in[2])
    c_y1 = []
    for k in range(1, NY):
        yt, dev = y_peer(k)
        c_y1.append(send(sx1.at[rows8(yt * 8, 8), :], wy1_in.at[k - 1], s_y1.at[k - 1], r_y1.at[k - 1], dev))

    for c in fs:
        c.wait_recv()
    a[:, :R] = gram_all[...]
    ii = lax.broadcasted_iota(jnp.int32, (R, R), 0)
    jj = lax.broadcasted_iota(jnp.int32, (R, R), 1)
    a[:, R:] = jnp.where(ii == jj, 1.0, 0.0).astype(F32)

    def factor(lo, hi):
        def body(k, carry):
            factor_step(k, a, rs)
            return carry
        lax.fori_loop(lo, hi, body, 0)

    for c in c_y2:
        c.wait_recv()
    acc = wt2[rows8(y * 32, 32), :]
    for k in range(NY - 1):
        acc = acc + wy2_in[k]
    sy2[...] = acc
    c_x2 = []
    for k in range(1, NX):
        xt, dev = x_peer(k)
        c_x2.append(send(sy2.at[rows8(xt * 8, 8), :], wx2_in.at[k - 1], s_x2.at[k - 1], r_x2.at[k - 1], dev))

    factor(0, 8)

    for c in c_y1:
        c.wait_recv()
    acc = sx1[rows8(y * 8, 8), :]
    for k in range(NY - 1):
        acc = acc + wy1_in[k]
    w1 = wf1.at[rows8(x * 64 + y * 8, 8), :]
    w1[...] = acc
    c_y1g = [send(w1, w1, s_y1g.at[k - 1], r_y1g.at[k - 1], y_peer(k)[1]) for k in range(1, NY)]
    for c in c_x2:
        c.wait_recv()
    w2 = wf2.at[rows8(y * 32 + x * 8, 8), :]
    w2[...] = (sy2[rows8(x * 8, 8), :] + wx2_in[0]) + (wx2_in[1] + wx2_in[2])
    c_x2g = [send(w2, w2, s_x2g.at[k - 1], r_x2g.at[k - 1], x_peer(k)[1]) for k in range(1, NX)]

    factor(8, 16)

    for c in c_x2g:
        c.wait_recv()
    w2 = wf2.at[rows8(y * 32, 32), :]
    c_y2g = [send(w2, w2, s_y2g.at[k - 1], r_y2g.at[k - 1], y_peer(k)[1]) for k in range(1, NY)]
    for c in c_y1g:
        c.wait_recv()
    w1 = wf1.at[rows8(x * 64, 64), :]
    c_x1g = [send(w1, w1, s_x1g.at[k - 1], r_x1g.at[k - 1], x_peer(k)[1]) for k in range(1, NX)]

    factor(16, 32)

    inv = a[:, R:]
    ortho = dot(power[...], inv, ((1,), (1,)))
    for c in c_y2g:
        c.wait_recv()
    for c in c_x1g:
        c.wait_recv()
    right[:, :CUT] = dot(inv, wf1[...], ((1,), (0,)))
    right[:, CUT:] = dot(inv, wf2[...], ((1,), (0,)))
    sq[col] = dot(jnp.ones((8, WIDE), F32), right[...] * right[...], ((1,), (1,)))
    cs = [send(sq.at[col], sq.at[col], s_sq.at[k - 1], r_sq.at[k - 1], col_peer(k)) for k in range(1, 2 * NZ)]

    nm_ref[...] = buf[:, :COLS] - (1.0 - KEEP_RATE) * dot(ortho, right[:, :COLS], ((1,), (0,)))

    for c in cs:
        c.wait_recv()
    squares = sq[0]
    for k in range(1, 2 * NZ):
        squares = squares + sq[k]
    norms = jnp.sqrt(squares[:1]) + NORM_EPS
    nb_ref[...] = right[...].T[:COLS] / norms
    up_ref[...] = (math.sqrt(M * N / R) * dot(ortho / norms, right[:, :COLS], ((1,), (0,)))).astype(BF16)

    for c in sent:
        c.wait_send()


def shards(momentum, gradient, basis):
    vmem = pl.BlockSpec(memory_space=pltpu.VMEM)
    v = lambda *s: pltpu.VMEM(s, F32)
    d = pltpu.SemaphoreType.DMA
    sems = []
    for n in (0, 7, 7, 8, 3, 7, 7, 8, 3, 7, 7, 3, 7, 3, 3, 7, 15):
        sems += [d(()) if n == 0 else d((n,))] * 2
    return pl.pallas_call(
        kernel,
        out_shape=(
            jax.ShapeDtypeStruct((ROWS, COLS), F32),
            jax.ShapeDtypeStruct((COLS, R), F32),
            jax.ShapeDtypeStruct((ROWS, COLS), BF16),
        ),
        in_specs=[vmem] * 3,
        out_specs=(vmem,) * 3,
        scratch_shapes=[
            v(ROWS, WIDE), v(ROWS, R), v(128, R), v(128, R), v(7, 16, R), v(ROWS, R),
            v(R, R), v(NX, 16, R), v(NY, 16, R), v(R, R),
            v(R, CUT), v(R, REST), v(3, 64, CUT), v(64, CUT), v(7, 8, CUT),
            v(7, 32, REST), v(32, REST), v(3, 8, REST), v(R, CUT), v(R, REST),
            v(R, 2 * R), v(8, 2 * R), v(R, WIDE), v(2 * NZ, 8, R),
            *sems,
        ],
        compiler_params=pltpu.CompilerParams(
            collective_id=0, has_side_effects=True, vmem_limit_bytes=48 << 20
        ),
    )(momentum, gradient, basis)


def solution(mesh):
    return jax.shard_map(
        shards,
        mesh=mesh,
        in_specs=(P("row", "col"), P("row", "col"), P("col", None)),
        out_specs=(P("row", "col"), P("col", None), P("row", "col")),
        check_vma=False,
    )
```

time: 548 us -> 87.9 us (0.16)
  waiting for transfers between devices: 429 us -> 0 us
  Pallas kernels: 0 us -> 79.6 us
  other arithmetic: 55.1 us -> 0 us
  blocking collectives: 29.4 us -> 0 us
  between operations: 15.2 us -> 0.69 us
  matrix products: 12.6 us -> 0 us
    psum x3 -> x0, waiting for transfers between devices: 429 us -> none  [the longest x1 156 us: shards(): right = lax.psum(local_right, 'row')]
    pallas_call x0 -> x1, Pallas kernels: none -> 79.6 us  [shards(): pl.pallas_call(kernel, out_shape=(jax.ShapeDtypeStruct((ROWS, COLS), F32)...]
    another operation x9 -> x0, other arithmetic: 53.7 us -> none  [the longest x6 34 us: shards(): lower = jnp.linalg.cholesky(gram)]
    psum x1 -> x0, blocking collectives: 29.4 us -> none  [shards(): squares = lax.psum(jnp.sum(right * right, axis=0), 'col')]
    dot_general x5 -> x0, matrix products: 11.1 us -> none  [the longest x1 3.6 us: shards(): jnp.dot(buffer, basis, precision=high, preferred_element_type=jnp.float32)]
  transfers between devices with their start and end apart: 3 -> 0, of which waited for: 3 -> 0; matrix products, arithmetic and copies ran while one was open for 0% -> 0% of each run, Pallas kernels for 0% -> 0%
where the time goes in v1:
time: 87.9 us; the launch traced here: 87.7 us
  Pallas kernels  79.6 us (91%)
  local copies, waits for them, and re-layouts  7.48 us (9%)
    pallas_call x1, Pallas kernels, shards(): pl.pallas_call(kernel, out_shape=(jax.ShapeDtypeStruct((ROWS, COLS), F32)...  79.6 us
    unnamed x15, local copies, waits for them, and re-layouts  5.34 us
    pallas_call x2, local copies, waits for them, and re-layouts, shards(): pl.pallas_call(kernel, out_shape=(jax.ShapeDtypeStruct((ROWS, COLS), F32)...  2.14 us

profile of v1, /device:TPU:1, one launch (start us, length us, event | category | flops | bytes accessed | tf_op | source)
XLA Modules:
  0.0 87.7 jit_solution(9543563379040330155)
XLA Ops:
  0.6 0.0 copy-start.5
  0.6 1.3 %copy.7.grad_ref = bf16[256,832]{1,0:T(8,128)(2,1)S(1)} copy(bf16[256,832]{0,1:T(8,128)(2,1)} %param.4) | data formatting | bytes 851968 | tf_op args[1]
  2.0 0.0 copy-done.5
  2.0 0.0 copy-start
  2.0 0.3 copy.6.mom_ref
  2.3 0.8 copy-done
  3.1 79.6 %shard_map.58 = (f32[256,832]{1,0:T(8,128)S(1)}, f32[832,256]{1,0:T(8,128)S(1)}, bf16[256,832]{1,0:T(8,128)(2,1)S(1)}) custom-call(f32[256,832]{1,0:T(8,128)S(1)} %copy.6.mom_ref, bf16[256,832]{1,0:T(8,128)(2,1)S(1)} %copy.7.grad_ref, f32[832,256]{1,0:T(8,128)S(1)} %copy-done), custom_call_target="tpu_custom_call" | custom-call | tf_op jit(solution)/shard_map/pallas_call | solution.py:282
  82.7 0.0 copy-start.1
  82.7 0.9 %copy-done.1 = f32[832,256]{1,0:T(8,128)} copy-done((f32[832,256]{1,0:T(8,128)}, f32[832,256]{1,0:T(8,128)S(1)}, u32[]{:S(2)}) %copy-start.1) | copy-done | bytes 851992
  83.6 0.0 copy-start.3
  83.6 0.8 copy-done.3
  84.4 0.0 copy-start.4
  84.4 1.2 %copy.8 = f32[256,832]{0,1:T(8,128)} copy(f32[256,832]{1,0:T(8,128)S(1)} %get-tuple-element.3) | data formatting | bytes 1703936 | tf_op jit(solution)/shard_map/pallas_call | solution.py:282
  85.6 0.0 copy-done.4
  85.6 0.0 copy-start.2
  85.6 1.0 %copy.9 = bf16[256,832]{0,1:T(8,128)(2,1)} copy(bf16[256,832]{1,0:T(8,128)(2,1)S(1)} %copy-done.4) | data formatting | bytes 851968 | tf_op jit(solution)/shard_map/pallas_call | solution.py:282
  86.5 0.3 copy-done.2
  86.8 0.9 %copy.11 = f32[832,256]{1,0:T(8,128)} copy(f32[832,256]{1,0:T(8,128)S(1)} %copy-done.2) | data formatting | bytes 1703936
Async XLA Ops:
  0.6 1.3 %copy-start.5 = (f32[256,832]{0,1:T(8,128)S(1)}, f32[256,832]{0,1:T(8,128)}, u32[]{:S(2)}) copy-start(f32[256,832]{0,1:T(8,128)} %param.3) | copy-start | bytes 2555908
  2.0 1.2 %copy-start = (f32[832,256]{1,0:T(8,128)S(1)}, f32[832,256]{1,0:T(8,128)}, u32[]{:S(2)}) copy-start(f32[832,256]{1,0:T(8,128)} %basis_ref.1) | copy-start | bytes 2555908
  82.7 0.9 %copy-start.1 = (f32[832,256]{1,0:T(8,128)}, f32[832,256]{1,0:T(8,128)S(1)}, u32[]{:S(2)}) copy-start(f32[832,256]{1,0:T(8,128)S(1)} %get-tuple-element.10) | copy-start | bytes 2555908
  83.6 0.8 copy-start.3
  84.4 1.2 %copy-start.4 = (bf16[256,832]{1,0:T(8,128)(2,1)S(1)}, bf16[256,832]{1,0:T(8,128)(2,1)}, u32[]{:S(2)}) copy-start(bf16[256,832]{1,0:T(8,128)(2,1)} %copy-done.3) | copy-start | bytes 1277956
  85.6 1.3 %copy-start.2 = (f32[832,256]{1,0:T(8,128)S(1)}, f32[832,256]{1,0:T(8,128)}, u32[]{:S(2)}) copy-start(f32[832,256]{1,0:T(8,128)} %copy-done.1) | copy-start | bytes 2555908

commit v2 on v1

v2 whole, which is shorter than its diff:
```python
import functools
import math

import jax
import jax.numpy as jnp
from jax import lax
from jax.experimental import pallas as pl
from jax.experimental.pallas import tpu as pltpu
from jax.sharding import PartitionSpec as P

M = 8192
N = 13312
R = 256
KEEP_RATE = 0.95
NORM_EPS = 1e-06

NX, NY, NZ = 4, 8, 8
ROWS = M // (NX * NY)
COLS = N // (2 * NZ)
CUT = 512
FIRST = CUT // NX
SMALL = FIRST // NY
SECOND = (COLS - CUT) // NY
F32 = jnp.float32
BF16 = jnp.bfloat16
MESH = pl.DeviceIdType.MESH


def dot(a, b, dims):
    return lax.dot_general(
        a, b, (dims, ((), ())), precision=lax.Precision.HIGHEST, preferred_element_type=F32
    )


def dot3(a, b, dims):
    ah = a.astype(BF16)
    bh = b.astype(BF16)
    al = (a - ah.astype(F32)).astype(BF16)
    bl = (b - bh.astype(F32)).astype(BF16)
    one = lambda p, q: lax.dot_general(p, q, (dims, ((), ())), preferred_element_type=F32)
    return one(ah, bh) + (one(ah, bl) + one(al, bh))


def factor_step(k, a, rs):
    off = pl.multiple_of(k * 8, 8)
    diag = pltpu.roll(a[pl.ds(off, 8), :R], lax.rem(R - off, R), 1)[:, :128]
    s = {}
    for j in range(8):
        col = jnp.broadcast_to(diag[:, j : j + 1], (8, 128))
        for i in range(j, 8):
            s[i, j] = jnp.broadcast_to(col[i : i + 1, :], (8, 128))
    rows = [a[pl.ds(off + i, 1), :] for i in range(8)]
    for j in range(8):
        d = lax.rsqrt(s[j, j])
        rows[j] = rows[j] * jnp.concatenate([d[:1]] * 4, axis=1)
        rs[j : j + 1, :] = rows[j]
        l = {i: s[i, j] * d for i in range(j + 1, 8)}
        for i in range(j + 1, 8):
            rows[i] = rows[i] - jnp.concatenate([l[i][:1]] * 4, axis=1) * rows[j]
            for c in range(j + 1, i + 1):
                s[i, c] = s[i, c] - l[i] * l[c]
    r = rs[...]
    a[pl.ds(off, 8), R:] = r[:, R:]
    hi = r.astype(BF16).astype(F32)
    mi = (r - hi).astype(BF16).astype(F32)
    lo = r - hi - mi
    lane = lax.broadcasted_iota(jnp.int32, (48, R), 1)
    lhs = jnp.concatenate([hi, hi, mi, mi, hi, lo], axis=0)[:, :R]
    lhs = jnp.where(lane >= off + 8, lhs, 0.0).astype(BF16)
    rhs = jnp.concatenate([hi, mi, hi, mi, lo, hi], axis=0).astype(BF16)
    a[...] = a[...] - lax.dot_general(
        lhs, rhs, (((0,), (0,)), ((), ())), preferred_element_type=F32
    )


def kernel(
    mom_hbm, grad_hbm, basis_hbm,
    nm_ref, right_ref, ortho_ref, norms_ref,
    mom_ref, grad_ref, basis_ref, buf, part, core_in, half, z_in, power,
    gram, gx, gy, gram_all,
    wt, wx1_in, sx1, wy1_in, wy2_in, sy2, wx2_in, wx3_in, wf,
    a, rs, sq,
    s_core, r_core, s_zr, r_zr, s_zg, r_zg, s_cg, r_cg,
    s_gx, r_gx, s_gy, r_gy, s_gz, r_gz, s_gc, r_gc,
    s_x1, r_x1, s_y1, r_y1, s_y2, r_y2, s_x2, r_x2, s_x3, r_x3,
    s_y1g, r_y1g, s_x1g, r_x1g, s_x2g, r_x2g, s_y2g, r_y2g,
    s_sq, r_sq, s_in,
):
    loads = [
        pltpu.make_async_copy(src, dst, s_in.at[i])
        for i, (src, dst) in enumerate(((mom_hbm, mom_ref), (grad_hbm, grad_ref), (basis_hbm, basis_ref)))
    ]
    for load in loads:
        load.start()
    row = lax.axis_index("row")
    col = lax.axis_index("col")
    x, y = row // NY, lax.rem(row, NY)
    z, core = col // 2, lax.rem(col, 2)

    def x_peer(k):
        xt = lax.rem(x + k, NX)
        return xt, (xt * NY + y, col)

    def y_peer(k):
        yt = lax.rem(y + k, NY)
        return yt, (x * NY + yt, col)

    def z_peer(k):
        zt = lax.rem(z + k, NZ)
        return zt, (row, zt * 2 + core)

    sibling = (row, z * 2 + 1 - core)

    def col_peer(k):
        return (row, lax.rem(col + k, 2 * NZ))

    sent = []

    def send(src, dst, ssem, rsem, dev):
        copy = pltpu.make_async_remote_copy(
            src_ref=src, dst_ref=dst, send_sem=ssem, recv_sem=rsem,
            device_id=dev, device_id_type=MESH,
        )
        copy.start()
        sent.append(copy)
        return copy

    def rows8(start, n):
        return pl.ds(pl.multiple_of(start, 8), n)

    barrier = pltpu.get_barrier_semaphore()
    peers = [x_peer(k)[1] for k in range(1, NX)]
    peers += [y_peer(k)[1] for k in range(1, NY)]
    peers += [col_peer(k) for k in range(1, 2 * NZ)]
    for dev in peers:
        pl.semaphore_signal(barrier, inc=1, device_id=dev, device_id_type=MESH)

    with jax.named_scope("partial_power"):
        for load in loads:
            load.wait()
        buf[...] = mom_ref[...] + grad_ref[...].astype(F32)
        part[...] = dot(buf[...], basis_ref[...], ((0,), (0,)))

    with jax.named_scope("entry"):
        pl.semaphore_wait(barrier, len(peers))

    with jax.named_scope("power_core"):
        c = send(part.at[rows8((1 - core) * 128, 128), :], core_in, s_core, r_core, sibling)
        c.wait_recv()
        half[...] = part[rows8(core * 128, 128), :] + core_in[...]
    with jax.named_scope("power_z"):
        cs = []
        for k in range(1, NZ):
            zt, dev = z_peer(k)
            cs.append(send(half.at[rows8(zt * 16, 16), :], z_in.at[k - 1], s_zr.at[k - 1], r_zr.at[k - 1], dev))
        total = half[rows8(z * 16, 16), :]
        for k in range(1, NZ):
            cs[k - 1].wait_recv()
            total = total + z_in[k - 1]

    mine16 = rows8(core * 128 + z * 16, 16)

    def gather_col(ref, ss, rr, sc, rc):
        mine = ref.at[mine16, :]
        cs = []
        for k in range(1, NZ):
            cs.append(send(mine, mine, ss.at[k - 1], rr.at[k - 1], z_peer(k)[1]))
        fs = [send(mine, mine, sc.at[0], rc.at[0], sibling)]
        for k in range(1, NZ):
            cs[k - 1].wait_recv()
            zs = lax.rem(z + NZ - k, NZ)
            theirs = ref.at[rows8(core * 128 + zs * 16, 16), :]
            fs.append(send(theirs, theirs, sc.at[k], rc.at[k], sibling))
        return fs

    with jax.named_scope("power_gather"):
        power[mine16, :] = total
        for c in gather_col(power, s_zg, r_zg, s_cg, r_cg):
            c.wait_recv()

    with jax.named_scope("gram_dot"):
        gram[...] = dot(power[...], power[...], ((0,), (0,)))
        cs = []
        for k in range(1, NX):
            cs.append(send(gram.at[mine16, :], gx.at[x], s_gx.at[k - 1], r_gx.at[k - 1], x_peer(k)[1]))
        gx[x] = gram[mine16, :]

    with jax.named_scope("w_dot_first"):
        wt[:CUT] = dot(buf[:CUT], power[...], ((1,), (0,)))
        c_x1 = []
        for k in range(1, NX):
            xt, dev = x_peer(k)
            c_x1.append(send(wt.at[rows8(xt * FIRST, FIRST), :], wx1_in.at[k - 1], s_x1.at[k - 1], r_x1.at[k - 1], dev))

    with jax.named_scope("gram_x"):
        for c in cs:
            c.wait_recv()
        gy[y] = (gx[0] + gx[1]) + (gx[2] + gx[3])
        cs = []
        for k in range(1, NY):
            cs.append(send(gy.at[y], gy.at[y], s_gy.at[k - 1], r_gy.at[k - 1], y_peer(k)[1]))

    with jax.named_scope("w_dot_second"):
        wt[CUT:] = dot(buf[CUT:], power[...], ((1,), (0,)))
        c_y2 = []
        for k in range(1, NY):
            yt, dev = y_peer(k)
            c_y2.append(send(wt.at[rows8(CUT + yt * SECOND, SECOND), :], wy2_in.at[k - 1], s_y2.at[k - 1], r_y2.at[k - 1], dev))

    with jax.named_scope("gram_y"):
        for c in cs:
            c.wait_recv()
        gram_all[mine16, :] = ((gy[0] + gy[1]) + (gy[2] + gy[3])) + ((gy[4] + gy[5]) + (gy[6] + gy[7]))
    with jax.named_scope("gram_gather"):
        fs = gather_col(gram_all, s_gz, r_gz, s_gc, r_gc)

    with jax.named_scope("w1_x"):
        for c in c_x1:
            c.wait_recv()
        sx1[...] = (wt[rows8(x * FIRST, FIRST), :] + wx1_in[0]) + (wx1_in[1] + wx1_in[2])
        c_y1 = []
        for k in range(1, NY):
            yt, dev = y_peer(k)
            c_y1.append(send(sx1.at[rows8(yt * SMALL, SMALL), :], wy1_in.at[k - 1], s_y1.at[k - 1], r_y1.at[k - 1], dev))

    with jax.named_scope("gram_wait"):
        for c in fs:
            c.wait_recv()
        a[:, :R] = gram_all[...]
        ii = lax.broadcasted_iota(jnp.int32, (R, R), 0)
        jj = lax.broadcasted_iota(jnp.int32, (R, R), 1)
        a[:, R:] = jnp.where(ii == jj, 1.0, 0.0).astype(F32)

    def factor(lo, hi):
        def body(k, carry):
            factor_step(k, a, rs)
            return carry
        lax.fori_loop(lo, hi, body, 0)

    with jax.named_scope("factor_0"):
        factor(0, 4)

    with jax.named_scope("w2_y"):
        for c in c_y2:
            c.wait_recv()
        acc = wt[rows8(CUT + y * SECOND, SECOND), :]
        for k in range(NY - 1):
            acc = acc + wy2_in[k]
        sy2[...] = acc
        c_x2 = []
        wx3_in[x] = acc[32:]
        for k in range(1, NX):
            xt, dev = x_peer(k)
            c_x2.append(send(sy2.at[rows8(xt * 8, 8), :], wx2_in.at[k - 1], s_x2.at[k - 1], r_x2.at[k - 1], dev))
            c_x2.append(send(sy2.at[pl.ds(32, 8), :], wx3_in.at[x], s_x3.at[k - 1], r_x3.at[k - 1], dev))

    with jax.named_scope("factor_1"):
        factor(4, 12)

    with jax.named_scope("w1_y"):
        for c in c_y1:
            c.wait_recv()
        acc = sx1[rows8(y * SMALL, SMALL), :]
        for k in range(NY - 1):
            acc = acc + wy1_in[k]
        w1 = wf.at[rows8(x * FIRST + y * SMALL, SMALL), :]
        w1[...] = acc
        c_y1g = [send(w1, w1, s_y1g.at[k - 1], r_y1g.at[k - 1], y_peer(k)[1]) for k in range(1, NY)]
    with jax.named_scope("w2_x"):
        for c in c_x2:
            c.wait_recv()
        w2 = wf.at[rows8(CUT + y * SECOND + x * 8, 8), :]
        w2[...] = (sy2[rows8(x * 8, 8), :] + wx2_in[0]) + (wx2_in[1] + wx2_in[2])
        c_x2g = [send(w2, w2, s_x2g.at[k - 1], r_x2g.at[k - 1], x_peer(k)[1]) for k in range(1, NX)]
        wf[rows8(CUT + y * SECOND + 32, 8), :] = (wx3_in[0] + wx3_in[1]) + (wx3_in[2] + wx3_in[3])

    with jax.named_scope("factor_2"):
        factor(12, 20)

    with jax.named_scope("w2_x_gather"):
        for c in c_x2g:
            c.wait_recv()
        w2 = wf.at[rows8(CUT + y * SECOND, SECOND), :]
        c_y2g = [send(w2, w2, s_y2g.at[k - 1], r_y2g.at[k - 1], y_peer(k)[1]) for k in range(1, NY)]
    with jax.named_scope("w1_y_gather"):
        for c in c_y1g:
            c.wait_recv()
        w1 = wf.at[rows8(x * FIRST, FIRST), :]
        c_x1g = [send(w1, w1, s_x1g.at[k - 1], r_x1g.at[k - 1], x_peer(k)[1]) for k in range(1, NX)]

    with jax.named_scope("factor_3"):
        factor(20, 32)

    with jax.named_scope("ortho"):
        inv = a[:, R:]
        ortho_ref[...] = dot(power[...], inv, ((1,), (1,)))
    with jax.named_scope("w_gather"):
        for c in c_y2g:
            c.wait_recv()
        for c in c_x1g:
            c.wait_recv()
    with jax.named_scope("right"):
        right_ref[...] = dot(wf[...], inv, ((1,), (1,)))
    with jax.named_scope("squares"):
        rt = right_ref[...]
        sums = jnp.sum((rt * rt).reshape(COLS // 8, 8, R), axis=0)
        sq[col] = jnp.sum(sums, axis=0, keepdims=True)
        cs = [send(sq.at[col], sq.at[col], s_sq.at[k - 1], r_sq.at[k - 1], col_peer(k)) for k in range(1, 2 * NZ)]

    with jax.named_scope("momentum"):
        nm_ref[...] = buf[...] - (1.0 - KEEP_RATE) * dot3(right_ref[...], ortho_ref[...], ((1,), (1,)))

    with jax.named_scope("norms"):
        for c in cs:
            c.wait_recv()
        squares = sq[0]
        for k in range(1, 2 * NZ):
            squares = squares + sq[k]
        norms_ref[...] = jnp.broadcast_to(jnp.sqrt(squares) + NORM_EPS, (8, R))

    with jax.named_scope("wait_sent"):
        for c in sent:
            c.wait_send()


def finish(nm_ref, right_ref, ortho_ref, norms_ref, nm_out, nb_out, up_out, nb, up, sems):
    c_nm = pltpu.make_async_copy(nm_ref, nm_out, sems.at[0])
    c_nm.start()
    nb[...] = right_ref[...] / norms_ref[:1]
    c_nb = pltpu.make_async_copy(nb, nb_out, sems.at[1])
    c_nb.start()
    up[...] = (math.sqrt(M * N / R) * dot3(nb[...], ortho_ref[...], ((1,), (1,)))).astype(BF16)
    c_up = pltpu.make_async_copy(up, up_out, sems.at[2])
    c_up.start()
    c_nm.wait()
    c_nb.wait()
    c_up.wait()


def shards(momentum, gradient, basis):
    vmem = pl.BlockSpec(memory_space=pltpu.VMEM)
    hbm = pl.BlockSpec(memory_space=pltpu.HBM)
    v = lambda *s: pltpu.VMEM(s, F32)
    d = pltpu.SemaphoreType.DMA
    sems = []
    for n in (0, 7, 7, 8, 3, 7, 7, 8, 3, 7, 7, 3, 3, 7, 3, 3, 7, 15):
        sems += [d(()) if n == 0 else d((n,))] * 2
    out = jax.ShapeDtypeStruct
    nm, right, ortho, norms = pl.pallas_call(
        kernel,
        out_shape=(out((COLS, ROWS), F32), out((COLS, R), F32), out((ROWS, R), F32), out((8, R), F32)),
        in_specs=[hbm] * 3,
        out_specs=(vmem,) * 4,
        scratch_shapes=[
            v(COLS, ROWS), pltpu.VMEM((COLS, ROWS), BF16), v(COLS, R),
            v(COLS, ROWS), v(ROWS, R), v(128, R), v(128, R), v(7, 16, R), v(ROWS, R),
            v(R, R), v(NX, 16, R), v(NY, 16, R), v(R, R),
            v(COLS, R), v(3, FIRST, R), v(FIRST, R), v(7, SMALL, R), v(7, SECOND, R), v(SECOND, R),
            v(3, 8, R), v(NX, 8, R), v(COLS, R),
            v(R, 2 * R), v(8, 2 * R), v(2 * NZ, 1, R),
            *sems, d((3,)),
        ],
        compiler_params=pltpu.CompilerParams(
            collective_id=0, has_side_effects=True, vmem_limit_bytes=40 << 20
        ),
    )(momentum.T, gradient.T, basis)
    nm, nb, up = pl.pallas_call(
        finish,
        out_shape=(out((COLS, ROWS), F32), out((COLS, R), F32), out((COLS, ROWS), BF16)),
        in_specs=[vmem] * 4,
        out_specs=(hbm,) * 3,
        scratch_shapes=[v(COLS, R), pltpu.VMEM((COLS, ROWS), BF16), d((3,))],
        compiler_params=pltpu.CompilerParams(vmem_limit_bytes=16 << 20),
    )(nm, right, ortho, norms)
    return nm.T, nb, up.T


def solution(mesh):
    return jax.shard_map(
        shards,
        mesh=mesh,
        in_specs=(P("row", "col"), P("row", "col"), P("col", None)),
        out_specs=(P("row", "col"), P("col", None), P("row", "col")),
        check_vma=False,
    )
```

time: 87.9 us -> 81.9 us (0.932)
  local copies, waits for them, and re-layouts: 7.48 us -> 3.31 us
  Pallas kernels: 79.6 us -> 77.6 us
    pallas_call x2 -> x0, local copies, waits for them, and re-layouts: 2.14 us -> none  [shards(): pl.pallas_call(kernel, out_shape=(jax.ShapeDtypeStruct((ROWS, COLS), F32)...]
    unnamed x15 -> x6, local copies, waits for them, and re-layouts: 5.34 us -> 3.31 us
    pallas_call x1 -> x2, Pallas kernels: 79.6 us -> 77.6 us  [the longest x1 76.3 us: shards(): pl.pallas_call(kernel, out_shape=(out((COLS, ROWS), F32), out((COLS, R),...]
where the time goes in v2:
time: 81.9 us; the launch traced here: 81.6 us
  Pallas kernels  77.6 us (95%)
  local copies, waits for them, and re-layouts  3.31 us (4%)
    pallas_call x1, Pallas kernels, shards(): pl.pallas_call(kernel, out_shape=(out((COLS, ROWS), F32), out((COLS, R),...  76.3 us
    unnamed x6, local copies, waits for them, and re-layouts  3.31 us

profile of v2, /device:TPU:1, one launch (start us, length us, event | category | flops | bytes accessed | tf_op | source)
XLA Modules:
  0.0 81.6 jit_solution(9137646274216071332)
XLA Ops:
  0.6 0.0 copy-start
  0.6 1.1 %copy-done = f32[256,832]{0,1:T(8,128)S(1)} copy-done((f32[256,832]{0,1:T(8,128)S(1)}, f32[256,832]{0,1:T(8,128)}, u32[]{:S(2)}) %copy-start) | copy-done | bytes 851992
  1.8 0.0 copy-start.1
  1.8 1.2 %copy-done.1 = f32[832,256]{1,0:T(8,128)S(1)} copy-done((f32[832,256]{1,0:T(8,128)S(1)}, f32[832,256]{1,0:T(8,128)}, u32[]{:S(2)}) %copy-start.1) | copy-done | bytes 851992
  2.9 0.0 copy-start.2
  2.9 1.0 %copy-done.2 = bf16[256,832]{0,1:T(8,128)(2,1)S(1)} copy-done((bf16[256,832]{0,1:T(8,128)(2,1)S(1)}, bf16[256,832]{0,1:T(8,128)(2,1)}, u32[]{:S(2)}) %copy-start.2) | copy-done | bytes 426008
  4.0 76.3 %shard_map.58 = (f32[832,256]{1,0:T(8,128)S(1)}, f32[832,256]{1,0:T(8,128)S(1)}, f32[256,256]{1,0:T(8,128)S(1)}, f32[8,256]{1,0:T(8,128)S(1)}) custom-call(f32[832,256]{1,0:T(8,128)S(1)} %bitcast.4, bf16[832,256]{1,0:T(8,128)(2,1)S(1)} %bitcast.5, f32[832,256]{1,0:T(8,128)S(1)} %copy-done.1), custom_call_target="tpu_custom_call" | custom-call | tf_op jit(solution)/shard_map/pallas_call | solution.py:349
  80.3 1.3 %shard_map.59 = (f32[832,256]{1,0:T(8,128)}, f32[832,256]{1,0:T(8,128)}, bf16[832,256]{1,0:T(8,128)(2,1)}) custom-call(f32[832,256]{1,0:T(8,128)S(1)} %get-tuple-element.10.nm_ref, f32[832,256]{1,0:T(8,128)S(1)} %get-tuple-element.11.right_ref, f32[256,256]{1,0:T(8,128)S(1)} %get-tuple-element.12.ortho_ref, f32[8,256]{1,0:T(8,128)S(1)} %get-tuple-element.13.norms_ref), custom_call_target="tpu_custom_call" | custom-call | tf_op jit(solution)/shard_map/pallas_call | solution.py:367
Async XLA Ops:
  0.6 1.2 %copy-start = (f32[256,832]{0,1:T(8,128)S(1)}, f32[256,832]{0,1:T(8,128)}, u32[]{:S(2)}) copy-start(f32[256,832]{0,1:T(8,128)} %param.3) | copy-start | bytes 2555908
  1.8 1.2 %copy-start.1 = (f32[832,256]{1,0:T(8,128)S(1)}, f32[832,256]{1,0:T(8,128)}, u32[]{:S(2)}) copy-start(f32[832,256]{1,0:T(8,128)} %basis_hbm.1) | copy-start | bytes 2555908
  2.9 1.0 %copy-start.2 = (bf16[256,832]{0,1:T(8,128)(2,1)S(1)}, bf16[256,832]{0,1:T(8,128)(2,1)}, u32[]{:S(2)}) copy-start(bf16[256,832]{0,1:T(8,128)(2,1)} %param.4) | copy-start | bytes 1277956

commit v3 on v2

v3 whole, which is shorter than its diff:
```python
import functools
import math

import jax
import jax.numpy as jnp
from jax import lax
from jax.experimental import pallas as pl
from jax.experimental.pallas import tpu as pltpu
from jax.sharding import PartitionSpec as P

M = 8192
N = 13312
R = 256
KEEP_RATE = 0.95
NORM_EPS = 1e-06

NX, NY, NZ = 4, 8, 8
ROWS = M // (NX * NY)
COLS = N // (2 * NZ)
CUT = 512
FIRST = CUT // NX
SMALL = FIRST // NY
SECOND = (COLS - CUT) // NY
PANEL = 32
FAR = (4, 3, 5, 2, 6, 1, 7)
NEAR = (1, 7, 2, 6, 3, 5, 4)
FAR_X = (2, 1, 3)
F32 = jnp.float32
BF16 = jnp.bfloat16
MESH = pl.DeviceIdType.MESH


def dot(a, b, dims):
    return lax.dot_general(
        a, b, (dims, ((), ())), precision=lax.Precision.HIGHEST, preferred_element_type=F32
    )


def dot3(a, b, dims):
    ah = a.astype(BF16)
    bh = b.astype(BF16)
    al = (a - ah.astype(F32)).astype(BF16)
    bl = (b - bh.astype(F32)).astype(BF16)
    one = lambda p, q: lax.dot_general(p, q, (dims, ((), ())), preferred_element_type=F32)
    return one(ah, bh) + (one(ah, bl) + one(al, bh))


def factor_panel(k, a):
    off = pl.multiple_of(k * PANEL, PANEL)
    base = pl.multiple_of(off // 128 * 128, 128)
    tiles = PANEL // 8
    sub = lax.broadcasted_iota(jnp.int32, (8, 128), 0)
    t = []
    for i in range(tiles):
        r = pl.ds(pl.multiple_of(off + 8 * i, 8), 8)
        row = a[r, :]
        own = pltpu.roll(a[r, pl.ds(base, 128)], lax.rem(128 - (off - base), 128), 1)
        t.append([own] + [row[:, 128 * q : 128 * q + 128] for q in range(4)])
    for b in range(tiles):
        cols = {}
        for i in range(b, tiles):
            for j in range(8):
                cols[i, j] = jnp.broadcast_to(t[i][0][:, 8 * b + j : 8 * b + j + 1], (8, 128))
        s = {}
        for j in range(8):
            for i in range(j, 8):
                s[i, j] = jnp.broadcast_to(cols[b, j][i : i + 1, :], (8, 128))
        scale = None
        for j in range(8):
            d = lax.rsqrt(s[j, j])
            l = {i: s[i, j] * d for i in range(j + 1, 8)}
            for m in range(j + 1, 8):
                for i in range(m, 8):
                    s[i, m] = s[i, m] - l[i] * l[m]
            pivot = [jnp.broadcast_to(t[b][q][j : j + 1, :], (8, 128)) * d for q in range(5)]
            for i in range(b, tiles):
                cols[i, j] = cols[i, j] * d
                for m in range(j + 1, 8):
                    cols[i, m] = cols[i, m] - cols[i, j] * l[m]
                times = cols[i, j] if i > b else jnp.where(sub > j, cols[i, j], 0.0)
                for q in range(5):
                    t[i][q] = t[i][q] - times * pivot[q]
            scale = d if j == 0 else jnp.where(sub == j, d, scale)
        for q in range(1, 5):
            t[b][q] = t[b][q] * scale
    r = jnp.concatenate([jnp.concatenate(t[i][1:], axis=1) for i in range(tiles)], axis=0)
    a[pl.ds(off, PANEL), R:] = r[:, R:]
    hi = r.astype(BF16).astype(F32)
    mi = (r - hi).astype(BF16).astype(F32)
    lo = r - hi - mi
    below = lax.broadcasted_iota(jnp.int32, (PANEL, R), 1) >= off + PANEL
    hl, ml, ll = (jnp.where(below, v[:, :R], 0.0).astype(BF16) for v in (hi, mi, lo))
    hr, mr, lr = hi.astype(BF16), mi.astype(BF16), lo.astype(BF16)
    lhs = jnp.concatenate([hl, hl, ml, ml, hl, ll], axis=0)
    rhs = jnp.concatenate([hr, mr, hr, mr, lr, hr], axis=0)
    a[...] = a[...] - lax.dot_general(
        lhs, rhs, (((0,), (0,)), ((), ())), preferred_element_type=F32
    )


def kernel(
    mom_hbm, grad_hbm, basis_hbm,
    nm_hbm, right_hbm, ortho_hbm, norms_hbm,
    nm_ref, right_ref, ortho_ref, norms_ref, mom_ref, grad_ref, basis_ref, buf, part, core_in, half, z_in, power,
    gram, gx, gy, gram_all,
    wt, wx1_in, sx1, wy1_in, wy2_in, sy2, wx2_in, wx3_in, wf,
    a, sq,
    s_core, r_core, s_zr, r_zr, s_zg, r_zg, s_cg, r_cg,
    s_gx, r_gx, s_gy, r_gy, s_gz, r_gz, s_gc, r_gc,
    s_x1, r_x1, s_y1, r_y1, s_y2, r_y2, s_x2, r_x2, s_x3, r_x3,
    s_y1g, r_y1g, s_x1g, r_x1g, s_x2g, r_x2g, s_y2g, r_y2g,
    s_sq, r_sq, s_in, s_out,
):
    loads = [
        pltpu.make_async_copy(src, dst, s_in.at[i])
        for i, (src, dst) in enumerate(((mom_hbm, mom_ref), (grad_hbm, grad_ref), (basis_hbm, basis_ref)))
    ]
    for load in loads:
        load.start()
    row = lax.axis_index("row")
    col = lax.axis_index("col")
    x, y = row // NY, lax.rem(row, NY)
    z, core = col // 2, lax.rem(col, 2)

    def x_peer(k):
        xt = lax.rem(x + k, NX)
        return xt, (xt * NY + y, col)

    def y_peer(k):
        yt = lax.rem(y + k, NY)
        return yt, (x * NY + yt, col)

    def z_peer(k):
        zt = lax.rem(z + k, NZ)
        return zt, (row, zt * 2 + core)

    sibling = (row, z * 2 + 1 - core)

    def col_peer(k):
        return (row, lax.rem(col + k, 2 * NZ))

    sent = []

    def send(src, dst, ssem, rsem, dev):
        copy = pltpu.make_async_remote_copy(
            src_ref=src, dst_ref=dst, send_sem=ssem, recv_sem=rsem,
            device_id=dev, device_id_type=MESH,
        )
        copy.start()
        sent.append(copy)
        return copy

    def rows8(start, n):
        return pl.ds(pl.multiple_of(start, 8), n)

    barrier = pltpu.get_barrier_semaphore()
    peers = [x_peer(k)[1] for k in range(1, NX)]
    peers += [y_peer(k)[1] for k in range(1, NY)]
    peers += [col_peer(k) for k in range(1, 2 * NZ)]
    for dev in peers:
        pl.semaphore_signal(barrier, inc=1, device_id=dev, device_id_type=MESH)

    ii = lax.broadcasted_iota(jnp.int32, (R, R), 0)
    jj = lax.broadcasted_iota(jnp.int32, (R, R), 1)
    a[:, R:] = jnp.where(ii == jj, 1.0, 0.0).astype(F32)

    mine128 = rows8(core * 128, 128)
    theirs128 = rows8((1 - core) * 128, 128)
    mine16 = rows8(core * 128 + z * 16, 16)

    def part_power(half_core):
        lanes = pl.ds(pl.multiple_of(half_core * 128, 128), 128)
        return dot(buf[:, lanes], basis_ref[...], ((0,), (0,)))

    def send_all(order, peer, src, dst, ss, rr):
        out = {}
        for k in order:
            at, dev = peer(k)
            out[k] = send(src(at), dst(k), ss.at[k - 1], rr.at[k - 1], dev)
        return out

    with jax.named_scope("partial_power"):
        for load in loads:
            load.wait()
        buf[...] = mom_ref[...] + grad_ref[...].astype(F32)
        part[theirs128, :] = part_power(1 - core)
        pl.semaphore_wait(barrier, len(peers))
        c = send(part.at[theirs128, :], core_in, s_core, r_core, sibling)
        part[mine128, :] = part_power(core)

    with jax.named_scope("power_sum"):
        c.wait_recv()
        half[...] = part[mine128, :] + core_in[...]
        cs = send_all(FAR, z_peer, lambda zt: half.at[rows8(zt * 16, 16), :], lambda k: z_in.at[k - 1], s_zr, r_zr)
        total = half[rows8(z * 16, 16), :]
        for k in NEAR:
            cs[k].wait_recv()
            total = total + z_in[k - 1]

    def gather_z(ref, ss, rr, sc, rc):
        mine = ref.at[mine16, :]
        cs = send_all(FAR, z_peer, lambda zt: mine, lambda k: mine, ss, rr)
        return cs, [send(mine, mine, sc.at[0], rc.at[0], sibling)]

    def gather_core(ref, cs, fs, sc, rc):
        for k in NEAR:
            cs[k].wait_recv()
            zs = lax.rem(z + NZ - k, NZ)
            theirs = ref.at[rows8(core * 128 + zs * 16, 16), :]
            fs.append(send(theirs, theirs, sc.at[k], rc.at[k], sibling))

    with jax.named_scope("power_gather"):
        power[mine16, :] = total
        cs, fs = gather_z(power, s_zg, r_zg, s_cg, r_cg)
        gather_core(power, cs, fs, s_cg, r_cg)
        for c in fs:
            c.wait_recv()

    with jax.named_scope("gram_dot"):
        gram[...] = dot(power[...], power[...], ((0,), (0,)))
        gx[x] = gram[mine16, :]
        c_gx = send_all(FAR_X, x_peer, lambda xt: gx.at[x], lambda k: gx.at[x], s_gx, r_gx)

    with jax.named_scope("w_dot"):
        wt[:CUT] = dot(buf[:CUT], power[...], ((1,), (0,)))
        c_x1 = send_all(FAR_X, x_peer, lambda xt: wt.at[rows8(xt * FIRST, FIRST), :], lambda k: wx1_in.at[k - 1], s_x1, r_x1)
        wt[CUT:] = dot(buf[CUT:], power[...], ((1,), (0,)))

    with jax.named_scope("gram_x"):
        for c in c_gx.values():
            c.wait_recv()
        gy[y] = (gx[0] + gx[1]) + (gx[2] + gx[3])
        c_gy = send_all(FAR, y_peer, lambda yt: gy.at[y], lambda k: gy.at[y], s_gy, r_gy)
        c_y2 = send_all(
            FAR, y_peer, lambda yt: wt.at[rows8(CUT + yt * SECOND, SECOND), :], lambda k: wy2_in.at[k - 1], s_y2, r_y2
        )

    with jax.named_scope("gram_y"):
        for c in c_gy.values():
            c.wait_recv()
        gram_all[mine16, :] = ((gy[0] + gy[1]) + (gy[2] + gy[3])) + ((gy[4] + gy[5]) + (gy[6] + gy[7]))
        c_gz, fs = gather_z(gram_all, s_gz, r_gz, s_gc, r_gc)

    with jax.named_scope("w1_x"):
        for c in c_x1.values():
            c.wait_recv()
        sx1[...] = (wt[rows8(x * FIRST, FIRST), :] + wx1_in[0]) + (wx1_in[1] + wx1_in[2])
        c_y1 = send_all(FAR, y_peer, lambda yt: sx1.at[rows8(yt * SMALL, SMALL), :], lambda k: wy1_in.at[k - 1], s_y1, r_y1)

    with jax.named_scope("w2_y"):
        for c in c_y2.values():
            c.wait_recv()
        acc = wt[rows8(CUT + y * SECOND, SECOND), :]
        for k in range(NY - 1):
            acc = acc + wy2_in[k]
        sy2[...] = acc
        wx3_in[x] = acc[32:]
        c_x2 = send_all(FAR_X, x_peer, lambda xt: sy2.at[rows8(xt * 8, 8), :], lambda k: wx2_in.at[k - 1], s_x2, r_x2)
        c_x3 = send_all(FAR_X, x_peer, lambda xt: sy2.at[pl.ds(32, 8), :], lambda k: wx3_in.at[x], s_x3, r_x3)

    with jax.named_scope("gram_z"):
        gather_core(gram_all, c_gz, fs, s_gc, r_gc)

    with jax.named_scope("w2_x"):
        for c in (*c_x2.values(), *c_x3.values()):
            c.wait_recv()
        w2 = wf.at[rows8(CUT + y * SECOND + x * 8, 8), :]
        w2[...] = (sy2[rows8(x * 8, 8), :] + wx2_in[0]) + (wx2_in[1] + wx2_in[2])
        c_x2g = send_all(FAR_X, x_peer, lambda xt: w2, lambda k: w2, s_x2g, r_x2g)
        wf[rows8(CUT + y * SECOND + 32, 8), :] = (wx3_in[0] + wx3_in[1]) + (wx3_in[2] + wx3_in[3])
    with jax.named_scope("w1_y"):
        for c in c_y1.values():
            c.wait_recv()
        acc = sx1[rows8(y * SMALL, SMALL), :]
        for k in range(NY - 1):
            acc = acc + wy1_in[k]
        w1 = wf.at[rows8(x * FIRST + y * SMALL, SMALL), :]
        w1[...] = acc
        c_y1g = send_all(FAR, y_peer, lambda yt: w1, lambda k: w1, s_y1g, r_y1g)

    def factor(lo, hi):
        def body(k, carry):
            factor_panel(k, a)
            return carry
        lax.fori_loop(lo, hi, body, 0)

    with jax.named_scope("factor_0"):
        for c in fs:
            c.wait_recv()
        a[:, :R] = gram_all[...]
        factor(0, 1)

    with jax.named_scope("w2_x_gather"):
        for c in c_x2g.values():
            c.wait_recv()
        w2y = wf.at[rows8(CUT + y * SECOND, SECOND), :]
        c_y2g = send_all(FAR, y_peer, lambda yt: w2y, lambda k: w2y, s_y2g, r_y2g)
    with jax.named_scope("factor_1"):
        factor(1, 2)
    with jax.named_scope("w1_y_gather"):
        for c in c_y1g.values():
            c.wait_recv()
        w1x = wf.at[rows8(x * FIRST, FIRST), :]
        c_x1g = send_all(FAR_X, x_peer, lambda xt: w1x, lambda k: w1x, s_x1g, r_x1g)

    with jax.named_scope("factor_2"):
        factor(2, R // PANEL)

    def store(src, dst, i):
        copy = pltpu.make_async_copy(src, dst, s_out.at[i])
        copy.start()
        return copy

    with jax.named_scope("ortho"):
        ortho_ref[...] = dot3(power[...], a[:, R:], ((1,), (1,)))
        stores = [store(ortho_ref, ortho_hbm, 1)]
    with jax.named_scope("right"):
        for c in c_x1g.values():
            c.wait_recv()
        right_ref[:CUT] = dot3(wf[:CUT], a[:, R:], ((1,), (1,)))
        for c in c_y2g.values():
            c.wait_recv()
        right_ref[CUT:] = dot3(wf[CUT:], a[:, R:], ((1,), (1,)))
    with jax.named_scope("squares"):
        rt = right_ref[...]
        sums = jnp.sum((rt * rt).reshape(COLS // 8, 8, R), axis=0)
        sq[col] = jnp.sum(sums, axis=0, keepdims=True)
        cs = [
            send(sq.at[col], sq.at[col], s_sq.at[k - 1], r_sq.at[k - 1], col_peer(k))
            for k in (8, 7, 9, 6, 10, 5, 11, 4, 12, 3, 13, 2, 14, 1, 15)
        ]
        stores.append(store(right_ref, right_hbm, 0))

    with jax.named_scope("momentum"):
        nm_ref[...] = buf[...] - (1.0 - KEEP_RATE) * dot3(right_ref[...], ortho_ref[...], ((1,), (1,)))
        stores.append(store(nm_ref, nm_hbm, 2))

    with jax.named_scope("norms"):
        for c in cs:
            c.wait_recv()
        squares = sq[0]
        for k in range(1, 2 * NZ):
            squares = squares + sq[k]
        norms_ref[...] = jnp.broadcast_to(jnp.sqrt(squares) + NORM_EPS, (8, R))
        stores.append(store(norms_ref, norms_hbm, 3))

    with jax.named_scope("wait_sent"):
        for c in stores:
            c.wait()
        for c in sent:
            c.wait_send()


def finish(nm_in, right_in, ortho_in, norms_in, nm_out, nb_out, up_out, nm, right, ortho, norms, nb, up, sems):
    def copy(i, src, dst):
        c = pltpu.make_async_copy(src, dst, sems.at[i])
        c.start()
        return c

    c_norms = copy(0, norms_in, norms)
    c_right = copy(1, right_in, right)
    c_ortho = copy(2, ortho_in, ortho)
    c_nm = copy(3, nm_in, nm)
    c_norms.wait()
    c_right.wait()
    nb[...] = right[...] / norms[:1]
    out = [copy(4, nb, nb_out)]
    c_nm.wait()
    out.append(copy(5, nm, nm_out))
    c_ortho.wait()
    up[...] = (math.sqrt(M * N / R) * dot3(nb[...], ortho[...], ((1,), (1,)))).astype(BF16)
    out.append(copy(6, up, up_out))
    for c in out:
        c.wait()


def shards(momentum, gradient, basis):
    hbm = pl.BlockSpec(memory_space=pltpu.HBM)
    v = lambda *s: pltpu.VMEM(s, F32)
    d = pltpu.SemaphoreType.DMA
    sems = []
    for n in (0, 7, 7, 8, 3, 7, 7, 8, 3, 7, 7, 3, 3, 7, 3, 3, 7, 15):
        sems += [d(()) if n == 0 else d((n,))] * 2
    out = jax.ShapeDtypeStruct
    nm, right, ortho, norms = pl.pallas_call(
        kernel,
        out_shape=(out((COLS, ROWS), F32), out((COLS, R), F32), out((ROWS, R), F32), out((8, R), F32)),
        in_specs=[hbm] * 3,
        out_specs=(hbm,) * 4,
        scratch_shapes=[
            v(COLS, ROWS), v(COLS, R), v(ROWS, R), v(8, R),
            v(COLS, ROWS), pltpu.VMEM((COLS, ROWS), BF16), v(COLS, R),
            v(COLS, ROWS), v(ROWS, R), v(128, R), v(128, R), v(7, 16, R), v(ROWS, R),
            v(R, R), v(NX, 16, R), v(NY, 16, R), v(R, R),
            v(COLS, R), v(3, FIRST, R), v(FIRST, R), v(7, SMALL, R), v(7, SECOND, R), v(SECOND, R),
            v(3, 8, R), v(NX, 8, R), v(COLS, R),
            v(R, 2 * R), v(2 * NZ, 1, R),
            *sems, d((3,)), d((4,)),
        ],
        compiler_params=pltpu.CompilerParams(
            collective_id=0, has_side_effects=True, vmem_limit_bytes=58 << 20
        ),
    )(momentum.T, gradient.T, basis)
    nm, nb, up = pl.pallas_call(
        finish,
        out_shape=(out((COLS, ROWS), F32), out((COLS, R), F32), out((COLS, ROWS), BF16)),
        in_specs=[hbm] * 4,
        out_specs=(hbm,) * 3,
        scratch_shapes=[v(COLS, ROWS), v(COLS, R), v(ROWS, R), v(8, R), v(COLS, R), pltpu.VMEM((COLS, ROWS), BF16), d((7,))],
        compiler_params=pltpu.CompilerParams(vmem_limit_bytes=58 << 20),
    )(nm, right, ortho, norms)
    return nm.T, nb, up.T


def solution(mesh):
    return jax.shard_map(
        shards,
        mesh=mesh,
        in_specs=(P("row", "col"), P("row", "col"), P("col", None)),
        out_specs=(P("row", "col"), P("col", None), P("row", "col")),
        check_vma=False,
    )
```

time: 81.9 us -> 74.6 us (0.911)
  Pallas kernels: 77.6 us -> 73.8 us
  local copies, waits for them, and re-layouts: 3.31 us -> 0 us
    pallas_call x1, Pallas kernels: 76.3 us -> 70.9 us  [shards(): pl.pallas_call(kernel, out_shape=(out((COLS, ROWS), F32), out((COLS, R),...]
    unnamed x6 -> x0, local copies, waits for them, and re-layouts: 3.31 us -> none
    pallas_call x1, Pallas kernels: 1.35 us -> 2.88 us  [shards(): pl.pallas_call(finish, out_shape=(out((COLS, ROWS), F32), out((COLS, R),...]
where the time goes in v3:
time: 74.6 us; the launch traced here: 74.4 us
  Pallas kernels  73.8 us (99%)
    pallas_call x1, Pallas kernels, shards(): pl.pallas_call(kernel, out_shape=(out((COLS, ROWS), F32), out((COLS, R),...  70.9 us
    pallas_call x1, Pallas kernels, shards(): pl.pallas_call(finish, out_shape=(out((COLS, ROWS), F32), out((COLS, R),...  2.88 us

profile of v3, /device:TPU:1, one launch (start us, length us, event | category | flops | bytes accessed | tf_op | source)
XLA Modules:
  0.0 74.4 jit_solution(9278587295619176739)
XLA Ops:
  0.6 70.9 %shard_map.58 = (f32[832,256]{1,0:T(8,128)}, f32[832,256]{1,0:T(8,128)}, f32[256,256]{1,0:T(8,128)}, f32[8,256]{1,0:T(8,128)}) custom-call(f32[832,256]{1,0:T(8,128)} %bitcast.4, bf16[832,256]{1,0:T(8,128)(2,1)} %bitcast.5, f32[832,256]{1,0:T(8,128)} %basis_hbm.1), custom_call_target="tpu_custom_call" | custom-call | tf_op jit(solution)/shard_map/pallas_call | solution.py:385
  71.6 2.9 %shard_map.59 = (f32[832,256]{1,0:T(8,128)}, f32[832,256]{1,0:T(8,128)}, bf16[832,256]{1,0:T(8,128)(2,1)}) custom-call(f32[832,256]{1,0:T(8,128)} %get-tuple-element.10.nm_in, f32[832,256]{1,0:T(8,128)} %get-tuple-element.11.right_in, f32[256,256]{1,0:T(8,128)} %get-tuple-element.12.ortho_in, f32[8,256]{1,0:T(8,128)} %get-tuple-element.13.norms_in), custom_call_target="tpu_custom_call" | custom-call | tf_op jit(solution)/shard_map/pallas_call | solution.py:404

commit v4 on v3

--- a/solution.py
+++ b/solution.py
@@ -22,6 +22,7 @@
 SMALL = FIRST // NY
 SECOND = (COLS - CUT) // NY
 PANEL = 32
+KEPT = ((0, COLS), (COLS, COLS), (2 * COLS, ROWS), (2 * COLS + ROWS, 8))
 FAR = (4, 3, 5, 2, 6, 1, 7)
 NEAR = (1, 7, 2, 6, 3, 5, 4)
 FAR_X = (2, 1, 3)
@@ -100,8 +101,8 @@
 
 def kernel(
     mom_hbm, grad_hbm, basis_hbm,
-    nm_hbm, right_hbm, ortho_hbm, norms_hbm,
-    nm_ref, right_ref, ortho_ref, norms_ref, mom_ref, grad_ref, basis_ref, buf, part, core_in, half, z_in, power,
+    out_ref,
+    mom_ref, grad_ref, basis_ref, buf, part, core_in, half, z_in, power,
     gram, gx, gy, gram_all,
     wt, wx1_in, sx1, wy1_in, wy2_in, sy2, wx2_in, wx3_in, wf,
     a, sq,
@@ -109,8 +110,9 @@
     s_gx, r_gx, s_gy, r_gy, s_gz, r_gz, s_gc, r_gc,
     s_x1, r_x1, s_y1, r_y1, s_y2, r_y2, s_x2, r_x2, s_x3, r_x3,
     s_y1g, r_y1g, s_x1g, r_x1g, s_x2g, r_x2g, s_y2g, r_y2g,
-    s_sq, r_sq, s_in, s_out,
+    s_sq, r_sq, s_in,
 ):
+    nm_ref, right_ref, ortho_ref, norms_ref = (out_ref.at[pl.ds(at, n), :] for at, n in KEPT)
     loads = [
         pltpu.make_async_copy(src, dst, s_in.at[i])
         for i, (src, dst) in enumerate(((mom_hbm, mom_ref), (grad_hbm, grad_ref), (basis_hbm, basis_ref)))
@@ -216,30 +218,24 @@
         for c in fs:
             c.wait_recv()
 
+    with jax.named_scope("w_dot"):
+        wt[:CUT] = dot(buf[:CUT], power[...], ((1,), (0,)))
+        c_x1 = send_all(FAR_X, x_peer, lambda xt: wt.at[rows8(xt * FIRST, FIRST), :], lambda k: wx1_in.at[k - 1], s_x1, r_x1)
+        wt[CUT:] = dot(buf[CUT:], power[...], ((1,), (0,)))
+        c_y2 = send_all(
+            FAR, y_peer, lambda yt: wt.at[rows8(CUT + yt * SECOND, SECOND), :], lambda k: wy2_in.at[k - 1], s_y2, r_y2
+        )
+
     with jax.named_scope("gram_dot"):
         gram[...] = dot(power[...], power[...], ((0,), (0,)))
         gx[x] = gram[mine16, :]
         c_gx = send_all(FAR_X, x_peer, lambda xt: gx.at[x], lambda k: gx.at[x], s_gx, r_gx)
 
-    with jax.named_scope("w_dot"):
-        wt[:CUT] = dot(buf[:CUT], power[...], ((1,), (0,)))
-        c_x1 = send_all(FAR_X, x_peer, lambda xt: wt.at[rows8(xt * FIRST, FIRST), :], lambda k: wx1_in.at[k - 1], s_x1, r_x1)
-        wt[CUT:] = dot(buf[CUT:], power[...], ((1,), (0,)))
-
     with jax.named_scope("gram_x"):
         for c in c_gx.values():
             c.wait_recv()
         gy[y] = (gx[0] + gx[1]) + (gx[2] + gx[3])
         c_gy = send_all(FAR, y_peer, lambda yt: gy.at[y], lambda k: gy.at[y], s_gy, r_gy)
-        c_y2 = send_all(
-            FAR, y_peer, lambda yt: wt.at[rows8(CUT + yt * SECOND, SECOND), :], lambda k: wy2_in.at[k - 1], s_y2, r_y2
-        )
-
-    with jax.named_scope("gram_y"):
-        for c in c_gy.values():
-            c.wait_recv()
-        gram_all[mine16, :] = ((gy[0] + gy[1]) + (gy[2] + gy[3])) + ((gy[4] + gy[5]) + (gy[6] + gy[7]))
-        c_gz, fs = gather_z(gram_all, s_gz, r_gz, s_gc, r_gc)
 
     with jax.named_scope("w1_x"):
         for c in c_x1.values():
@@ -258,8 +254,11 @@
         c_x2 = send_all(FAR_X, x_peer, lambda xt: sy2.at[rows8(xt * 8, 8), :], lambda k: wx2_in.at[k - 1], s_x2, r_x2)
         c_x3 = send_all(FAR_X, x_peer, lambda xt: sy2.at[pl.ds(32, 8), :], lambda k: wx3_in.at[x], s_x3, r_x3)
 
-    with jax.named_scope("gram_z"):
-        gather_core(gram_all, c_gz, fs, s_gc, r_gc)
+    with jax.named_scope("gram_y"):
+        for c in c_gy.values():
+            c.wait_recv()
+        gram_all[mine16, :] = ((gy[0] + gy[1]) + (gy[2] + gy[3])) + ((gy[4] + gy[5]) + (gy[6] + gy[7]))
+        c_gz, fs = gather_z(gram_all, s_gz, r_gz, s_gc, r_gc)
 
     with jax.named_scope("w2_x"):
         for c in (*c_x2.values(), *c_x3.values()):
@@ -278,42 +277,38 @@
         w1[...] = acc
         c_y1g = send_all(FAR, y_peer, lambda yt: w1, lambda k: w1, s_y1g, r_y1g)
 
+    with jax.named_scope("gram_z"):
+        gather_core(gram_all, c_gz, fs, s_gc, r_gc)
+
     def factor(lo, hi):
         def body(k, carry):
             factor_panel(k, a)
             return carry
         lax.fori_loop(lo, hi, body, 0)
 
-    with jax.named_scope("factor_0"):
-        for c in fs:
-            c.wait_recv()
-        a[:, :R] = gram_all[...]
-        factor(0, 1)
-
     with jax.named_scope("w2_x_gather"):
         for c in c_x2g.values():
             c.wait_recv()
         w2y = wf.at[rows8(CUT + y * SECOND, SECOND), :]
         c_y2g = send_all(FAR, y_peer, lambda yt: w2y, lambda k: w2y, s_y2g, r_y2g)
-    with jax.named_scope("factor_1"):
-        factor(1, 2)
+
+    with jax.named_scope("factor_first"):
+        for c in fs:
+            c.wait_recv()
+        a[:, :R] = gram_all[...]
+        factor(0, 2)
+
     with jax.named_scope("w1_y_gather"):
         for c in c_y1g.values():
             c.wait_recv()
         w1x = wf.at[rows8(x * FIRST, FIRST), :]
         c_x1g = send_all(FAR_X, x_peer, lambda xt: w1x, lambda k: w1x, s_x1g, r_x1g)
 
-    with jax.named_scope("factor_2"):
+    with jax.named_scope("factor_rest"):
         factor(2, R // PANEL)
-
-    def store(src, dst, i):
-        copy = pltpu.make_async_copy(src, dst, s_out.at[i])
-        copy.start()
-        return copy
 
     with jax.named_scope("ortho"):
         ortho_ref[...] = dot3(power[...], a[:, R:], ((1,), (1,)))
-        stores = [store(ortho_ref, ortho_hbm, 1)]
     with jax.named_scope("right"):
         for c in c_x1g.values():
             c.wait_recv()
@@ -329,11 +324,9 @@
             send(sq.at[col], sq.at[col], s_sq.at[k - 1], r_sq.at[k - 1], col_peer(k))
             for k in (8, 7, 9, 6, 10, 5, 11, 4, 12, 3, 13, 2, 14, 1, 15)
         ]
-        stores.append(store(right_ref, right_hbm, 0))
 
     with jax.named_scope("momentum"):
         nm_ref[...] = buf[...] - (1.0 - KEEP_RATE) * dot3(right_ref[...], ortho_ref[...], ((1,), (1,)))
-        stores.append(store(nm_ref, nm_hbm, 2))
 
     with jax.named_scope("norms"):
         for c in cs:
@@ -342,34 +335,25 @@
         for k in range(1, 2 * NZ):
             squares = squares + sq[k]
         norms_ref[...] = jnp.broadcast_to(jnp.sqrt(squares) + NORM_EPS, (8, R))
-        stores.append(store(norms_ref, norms_hbm, 3))
 
     with jax.named_scope("wait_sent"):
-        for c in stores:
-            c.wait()
         for c in sent:
             c.wait_send()
 
 
-def finish(nm_in, right_in, ortho_in, norms_in, nm_out, nb_out, up_out, nm, right, ortho, norms, nb, up, sems):
+def finish(kept, nm_out, nb_out, up_out, nb, up, sems):
+    nm, right, ortho, norms = (kept.at[pl.ds(at, n), :] for at, n in KEPT)
+
     def copy(i, src, dst):
         c = pltpu.make_async_copy(src, dst, sems.at[i])
         c.start()
         return c
 
-    c_norms = copy(0, norms_in, norms)
-    c_right = copy(1, right_in, right)
-    c_ortho = copy(2, ortho_in, ortho)
-    c_nm = copy(3, nm_in, nm)
-    c_norms.wait()
-    c_right.wait()
+    out = [copy(0, nm, nm_out)]
     nb[...] = right[...] / norms[:1]
-    out = [copy(4, nb, nb_out)]
-    c_nm.wait()
-    out.append(copy(5, nm, nm_out))
-    c_ortho.wait()
+    out.append(copy(1, nb, nb_out))
     up[...] = (math.sqrt(M * N / R) * dot3(nb[...], ortho[...], ((1,), (1,)))).astype(BF16)
-    out.append(copy(6, up, up_out))
+    out.append(copy(2, up, up_out))
     for c in out:
         c.wait()
 
@@ -382,33 +366,33 @@
     for n in (0, 7, 7, 8, 3, 7, 7, 8, 3, 7, 7, 3, 3, 7, 3, 3, 7, 15):
         sems += [d(()) if n == 0 else d((n,))] * 2
     out = jax.ShapeDtypeStruct
-    nm, right, ortho, norms = pl.pallas_call(
+    vmem = pl.BlockSpec(memory_space=pltpu.VMEM)
+    kept = pl.pallas_call(
         kernel,
-        out_shape=(out((COLS, ROWS), F32), out((COLS, R), F32), out((ROWS, R), F32), out((8, R), F32)),
+        out_shape=out((2 * COLS + ROWS + 8, R), F32),
         in_specs=[hbm] * 3,
-        out_specs=(hbm,) * 4,
+        out_specs=vmem,
         scratch_shapes=[
-            v(COLS, ROWS), v(COLS, R), v(ROWS, R), v(8, R),
             v(COLS, ROWS), pltpu.VMEM((COLS, ROWS), BF16), v(COLS, R),
             v(COLS, ROWS), v(ROWS, R), v(128, R), v(128, R), v(7, 16, R), v(ROWS, R),
             v(R, R), v(NX, 16, R), v(NY, 16, R), v(R, R),
             v(COLS, R), v(3, FIRST, R), v(FIRST, R), v(7, SMALL, R), v(7, SECOND, R), v(SECOND, R),
             v(3, 8, R), v(NX, 8, R), v(COLS, R),
             v(R, 2 * R), v(2 * NZ, 1, R),
-            *sems, d((3,)), d((4,)),
+            *sems, d((3,)),
         ],
         compiler_params=pltpu.CompilerParams(
-            collective_id=0, has_side_effects=True, vmem_limit_bytes=58 << 20
+            collective_id=0, has_side_effects=True, vmem_limit_bytes=40 << 20
         ),
-    )(momentum.T, gradient.T, basis)
+    )(*(pltpu.with_memory_space_constraint(v, pltpu.HBM) for v in (momentum.T, gradient.T, basis)))
     nm, nb, up = pl.pallas_call(
         finish,
         out_shape=(out((COLS, ROWS), F32), out((COLS, R), F32), out((COLS, ROWS), BF16)),
-        in_specs=[hbm] * 4,
+        in_specs=[vmem],
         out_specs=(hbm,) * 3,
-        scratch_shapes=[v(COLS, ROWS), v(COLS, R), v(ROWS, R), v(8, R), v(COLS, R), pltpu.VMEM((COLS, ROWS), BF16), d((7,))],
-        compiler_params=pltpu.CompilerParams(vmem_limit_bytes=58 << 20),
-    )(nm, right, ortho, norms)
+        scratch_shapes=[v(COLS, R), pltpu.VMEM((COLS, ROWS), BF16), d((3,))],
+        compiler_params=pltpu.CompilerParams(vmem_limit_bytes=40 << 20),
+    )(kept)
     return nm.T, nb, up.T
 
 

time: 74.6 us -> 70.8 us (0.949)
  Pallas kernels: 73.8 us -> 70 us
    pallas_call x1, Pallas kernels: 70.9 us -> 68.6 us  [shards(): pl.pallas_call(kernel, out_shape=out((2 * COLS + ROWS + 8, R), F32), in_s...]
    pallas_call x1, Pallas kernels: 2.88 us -> 1.35 us  [shards(): pl.pallas_call(finish, out_shape=(out((COLS, ROWS), F32), out((COLS, R),...]
where the time goes in v4:
time: 70.8 us; the launch traced here: 70.6 us
  Pallas kernels  70 us (99%)
    pallas_call x1, Pallas kernels, shards(): pl.pallas_call(kernel, out_shape=out((2 * COLS + ROWS + 8, R), F32), in_s...  68.6 us

profile of v4, /device:TPU:1, one launch (start us, length us, event | category | flops | bytes accessed | tf_op | source)
XLA Modules:
  0.0 70.6 jit_solution(16532696155320483888)
XLA Ops:
  0.6 68.6 %shard_map.58.kept = f32[1928,256]{1,0:T(8,128)S(1)} custom-call(f32[832,256]{1,0:T(8,128)} %bitcast.4, bf16[832,256]{1,0:T(8,128)(2,1)} %bitcast.5, f32[832,256]{1,0:T(8,128)} %basis_hbm.1), custom_call_target="tpu_custom_call" | custom-call | tf_op jit(solution)/shard_map/pallas_call | solution.py:370
  69.3 1.3 %shard_map.59 = (f32[832,256]{1,0:T(8,128)}, f32[832,256]{1,0:T(8,128)}, bf16[832,256]{1,0:T(8,128)(2,1)}) custom-call(f32[1928,256]{1,0:T(8,128)S(1)} %shard_map.58.kept), custom_call_target="tpu_custom_call" | custom-call | tf_op jit(solution)/shard_map/pallas_call | solution.py:388

commit v5 on v4

--- a/solution.py
+++ b/solution.py
@@ -17,15 +17,16 @@
 NX, NY, NZ = 4, 8, 8
 ROWS = M // (NX * NY)
 COLS = N // (2 * NZ)
-CUT = 512
-FIRST = CUT // NX
-SMALL = FIRST // NY
-SECOND = (COLS - CUT) // NY
+CUT = (512, 768)
+FIRST = tuple(n // NX for n in CUT)
+SMALL = tuple(n // NY for n in FIRST)
+SECOND = tuple((COLS - n) // NY for n in CUT)
 PANEL = 32
 KEPT = ((0, COLS), (COLS, COLS), (2 * COLS, ROWS), (2 * COLS + ROWS, 8))
 FAR = (4, 3, 5, 2, 6, 1, 7)
 NEAR = (1, 7, 2, 6, 3, 5, 4)
 FAR_X = (2, 1, 3)
+HALVES = (0, 1)
 F32 = jnp.float32
 BF16 = jnp.bfloat16
 MESH = pl.DeviceIdType.MESH
@@ -181,104 +182,127 @@
             out[k] = send(src(at), dst(k), ss.at[k - 1], rr.at[k - 1], dev)
         return out
 
+    def arrive(copies):
+        for c in copies.values():
+            c.wait_recv()
+
     with jax.named_scope("partial_power"):
         for load in loads:
             load.wait()
         buf[...] = mom_ref[...] + grad_ref[...].astype(F32)
-        part[theirs128, :] = part_power(1 - core)
+        theirs = part_power(1 - core)
+        for h in HALVES:
+            part[h, theirs128, :] = theirs[:, 128 * h : 128 * h + 128]
         pl.semaphore_wait(barrier, len(peers))
-        c = send(part.at[theirs128, :], core_in, s_core, r_core, sibling)
-        part[mine128, :] = part_power(core)
-
-    with jax.named_scope("power_sum"):
-        c.wait_recv()
-        half[...] = part[mine128, :] + core_in[...]
-        cs = send_all(FAR, z_peer, lambda zt: half.at[rows8(zt * 16, 16), :], lambda k: z_in.at[k - 1], s_zr, r_zr)
-        total = half[rows8(z * 16, 16), :]
-        for k in NEAR:
-            cs[k].wait_recv()
-            total = total + z_in[k - 1]
+        c_core = [send(part.at[h, theirs128, :], core_in.at[h], s_core.at[h], r_core.at[h], sibling) for h in HALVES]
+        mine = part_power(core)
+
+    c_z = [None, None]
+    with jax.named_scope("power_core"):
+        for h in HALVES:
+            c_core[h].wait_recv()
+            half[h] = mine[:, 128 * h : 128 * h + 128] + core_in[h]
+            c_z[h] = send_all(
+                FAR, z_peer, lambda zt: half.at[h, rows8(zt * 16, 16), :], lambda k: z_in.at[h, k - 1], s_zr.at[h], r_zr.at[h]
+            )
 
     def gather_z(ref, ss, rr, sc, rc):
-        mine = ref.at[mine16, :]
-        cs = send_all(FAR, z_peer, lambda zt: mine, lambda k: mine, ss, rr)
-        return cs, [send(mine, mine, sc.at[0], rc.at[0], sibling)]
+        own = ref.at[mine16, :]
+        cs = send_all(FAR, z_peer, lambda zt: own, lambda k: own, ss, rr)
+        return cs, [send(own, own, sc.at[0], rc.at[0], sibling)]
 
     def gather_core(ref, cs, fs, sc, rc):
         for k in NEAR:
             cs[k].wait_recv()
             zs = lax.rem(z + NZ - k, NZ)
-            theirs = ref.at[rows8(core * 128 + zs * 16, 16), :]
-            fs.append(send(theirs, theirs, sc.at[k], rc.at[k], sibling))
-
-    with jax.named_scope("power_gather"):
-        power[mine16, :] = total
-        cs, fs = gather_z(power, s_zg, r_zg, s_cg, r_cg)
-        gather_core(power, cs, fs, s_cg, r_cg)
-        for c in fs:
-            c.wait_recv()
-
-    with jax.named_scope("w_dot"):
-        wt[:CUT] = dot(buf[:CUT], power[...], ((1,), (0,)))
-        c_x1 = send_all(FAR_X, x_peer, lambda xt: wt.at[rows8(xt * FIRST, FIRST), :], lambda k: wx1_in.at[k - 1], s_x1, r_x1)
-        wt[CUT:] = dot(buf[CUT:], power[...], ((1,), (0,)))
-        c_y2 = send_all(
-            FAR, y_peer, lambda yt: wt.at[rows8(CUT + yt * SECOND, SECOND), :], lambda k: wy2_in.at[k - 1], s_y2, r_y2
+            other = ref.at[rows8(core * 128 + zs * 16, 16), :]
+            fs.append(send(other, other, sc.at[k], rc.at[k], sibling))
+
+    c_zg, f_zg = [None, None], [None, None]
+    with jax.named_scope("power_z"):
+        for h in HALVES:
+            total = half[h, rows8(z * 16, 16), :]
+            for k in NEAR:
+                c_z[h][k].wait_recv()
+                total = total + z_in[h, k - 1]
+            power[h, mine16, :] = total
+            c_zg[h], f_zg[h] = gather_z(power.at[h], s_zg.at[h], r_zg.at[h], s_cg.at[h], r_cg.at[h])
+
+    def w_first(h):
+        wt[h, : CUT[h]] = dot(buf[: CUT[h]], power[h], ((1,), (0,)))
+        n = FIRST[h]
+        return send_all(
+            FAR_X, x_peer, lambda xt: wt.at[h, rows8(xt * n, n), :], lambda k: wx1_in.at[h, k - 1, pl.ds(0, n), :],
+            s_x1.at[h], r_x1.at[h],
         )
 
-    with jax.named_scope("gram_dot"):
-        gram[...] = dot(power[...], power[...], ((0,), (0,)))
-        gx[x] = gram[mine16, :]
-        c_gx = send_all(FAR_X, x_peer, lambda xt: gx.at[x], lambda k: gx.at[x], s_gx, r_gx)
-
-    with jax.named_scope("gram_x"):
-        for c in c_gx.values():
-            c.wait_recv()
-        gy[y] = (gx[0] + gx[1]) + (gx[2] + gx[3])
-        c_gy = send_all(FAR, y_peer, lambda yt: gy.at[y], lambda k: gy.at[y], s_gy, r_gy)
-
-    with jax.named_scope("w1_x"):
-        for c in c_x1.values():
-            c.wait_recv()
-        sx1[...] = (wt[rows8(x * FIRST, FIRST), :] + wx1_in[0]) + (wx1_in[1] + wx1_in[2])
-        c_y1 = send_all(FAR, y_peer, lambda yt: sx1.at[rows8(yt * SMALL, SMALL), :], lambda k: wy1_in.at[k - 1], s_y1, r_y1)
-
-    with jax.named_scope("w2_y"):
-        for c in c_y2.values():
-            c.wait_recv()
-        acc = wt[rows8(CUT + y * SECOND, SECOND), :]
+    def w_second_dot(h):
+        wt[h, CUT[h] :] = dot(buf[CUT[h] :], power[h], ((1,), (0,)))
+
+    def w_second(h):
+        n = SECOND[h]
+        return send_all(
+            FAR, y_peer, lambda yt: wt.at[h, rows8(CUT[h] + yt * n, n), :], lambda k: wy2_in.at[h, k - 1, pl.ds(0, n), :],
+            s_y2.at[h], r_y2.at[h],
+        )
+
+    def w1_x(h, got):
+        arrive(got)
+        n, m = FIRST[h], SMALL[h]
+        sx1[h, :n] = (wt[h, rows8(x * n, n), :] + wx1_in[h, 0, :n]) + (wx1_in[h, 1, :n] + wx1_in[h, 2, :n])
+        return send_all(
+            FAR, y_peer, lambda yt: sx1.at[h, rows8(yt * m, m), :], lambda k: wy1_in.at[h, k - 1, pl.ds(0, m), :],
+            s_y1.at[h], r_y1.at[h],
+        )
+
+    def w2_y(h, got):
+        arrive(got)
+        n = SECOND[h]
+        acc = wt[h, rows8(CUT[h] + y * n, n), :]
         for k in range(NY - 1):
-            acc = acc + wy2_in[k]
-        sy2[...] = acc
-        wx3_in[x] = acc[32:]
-        c_x2 = send_all(FAR_X, x_peer, lambda xt: sy2.at[rows8(xt * 8, 8), :], lambda k: wx2_in.at[k - 1], s_x2, r_x2)
-        c_x3 = send_all(FAR_X, x_peer, lambda xt: sy2.at[pl.ds(32, 8), :], lambda k: wx3_in.at[x], s_x3, r_x3)
-
-    with jax.named_scope("gram_y"):
-        for c in c_gy.values():
-            c.wait_recv()
-        gram_all[mine16, :] = ((gy[0] + gy[1]) + (gy[2] + gy[3])) + ((gy[4] + gy[5]) + (gy[6] + gy[7]))
-        c_gz, fs = gather_z(gram_all, s_gz, r_gz, s_gc, r_gc)
-
-    with jax.named_scope("w2_x"):
-        for c in (*c_x2.values(), *c_x3.values()):
-            c.wait_recv()
-        w2 = wf.at[rows8(CUT + y * SECOND + x * 8, 8), :]
-        w2[...] = (sy2[rows8(x * 8, 8), :] + wx2_in[0]) + (wx2_in[1] + wx2_in[2])
-        c_x2g = send_all(FAR_X, x_peer, lambda xt: w2, lambda k: w2, s_x2g, r_x2g)
-        wf[rows8(CUT + y * SECOND + 32, 8), :] = (wx3_in[0] + wx3_in[1]) + (wx3_in[2] + wx3_in[3])
-    with jax.named_scope("w1_y"):
-        for c in c_y1.values():
-            c.wait_recv()
-        acc = sx1[rows8(y * SMALL, SMALL), :]
+            acc = acc + wy2_in[h, k, :n]
+        sy2[h, :n] = acc
+        wx3_in[h, x] = acc[n - 8 :]
+        one = {}
+        if n > 8:
+            one = send_all(
+                FAR_X, x_peer, lambda xt: sy2.at[h, rows8(xt * 8, 8), :], lambda k: wx2_in.at[h, k - 1], s_x2.at[h], r_x2.at[h]
+            )
+        two = send_all(
+            FAR_X, x_peer, lambda xt: sy2.at[h, pl.ds(n - 8, 8), :], lambda k: wx3_in.at[h, x], s_x3.at[h], r_x3.at[h]
+        )
+        return one, two
+
+    def w1_y(h, got):
+        arrive(got)
+        n, m = FIRST[h], SMALL[h]
+        acc = sx1[h, rows8(y * m, m), :]
         for k in range(NY - 1):
-            acc = acc + wy1_in[k]
-        w1 = wf.at[rows8(x * FIRST + y * SMALL, SMALL), :]
-        w1[...] = acc
-        c_y1g = send_all(FAR, y_peer, lambda yt: w1, lambda k: w1, s_y1g, r_y1g)
-
-    with jax.named_scope("gram_z"):
-        gather_core(gram_all, c_gz, fs, s_gc, r_gc)
+            acc = acc + wy1_in[h, k, :m]
+        own = wf.at[h, rows8(x * n + y * m, m), :]
+        own[...] = acc
+        return send_all(FAR, y_peer, lambda yt: own, lambda k: own, s_y1g.at[h], r_y1g.at[h])
+
+    def w2_x(h, got):
+        arrive(got[0])
+        arrive(got[1])
+        n = SECOND[h]
+        wf[h, rows8(CUT[h] + y * n + n - 8, 8), :] = (wx3_in[h, 0] + wx3_in[h, 1]) + (wx3_in[h, 2] + wx3_in[h, 3])
+        if n == 8:
+            return {}
+        own = wf.at[h, rows8(CUT[h] + y * n + x * 8, 8), :]
+        own[...] = (sy2[h, rows8(x * 8, 8), :] + wx2_in[h, 0]) + (wx2_in[h, 1] + wx2_in[h, 2])
+        return send_all(FAR_X, x_peer, lambda xt: own, lambda k: own, s_x2g.at[h], r_x2g.at[h])
+
+    def w2_x_gather(h, got):
+        arrive(got)
+        own = wf.at[h, rows8(CUT[h] + y * SECOND[h], SECOND[h]), :]
+        return send_all(FAR, y_peer, lambda yt: own, lambda k: own, s_y2g.at[h], r_y2g.at[h])
+
+    def w1_y_gather(h, got):
+        arrive(got)
+        own = wf.at[h, rows8(x * FIRST[h], FIRST[h]), :]
+        return send_all(FAR_X, x_peer, lambda xt: own, lambda k: own, s_x1g.at[h], r_x1g.at[h])
 
     def factor(lo, hi):
         def body(k, carry):
@@ -286,36 +310,74 @@
             return carry
         lax.fori_loop(lo, hi, body, 0)
 
-    with jax.named_scope("w2_x_gather"):
-        for c in c_x2g.values():
+    with jax.named_scope("first_half"):
+        gather_core(power.at[0], c_zg[0], f_zg[0], s_cg.at[0], r_cg.at[0])
+        for c in f_zg[0]:
             c.wait_recv()
-        w2y = wf.at[rows8(CUT + y * SECOND, SECOND), :]
-        c_y2g = send_all(FAR, y_peer, lambda yt: w2y, lambda k: w2y, s_y2g, r_y2g)
-
-    with jax.named_scope("factor_first"):
+        x1_0 = w_first(0)
+        w_second_dot(0)
+        y2_0 = w_second(0)
+        gather_core(power.at[1], c_zg[1], f_zg[1], s_cg.at[1], r_cg.at[1])
+        for c in f_zg[1]:
+            c.wait_recv()
+
+    with jax.named_scope("gram_dot"):
+        whole = jnp.concatenate([power[0], power[1]], axis=1)
+        gram[...] = dot(whole, whole, ((0,), (0,)))
+        gx[x] = gram[mine16, :]
+        c_gx = send_all(FAR_X, x_peer, lambda xt: gx.at[x], lambda k: gx.at[x], s_gx, r_gx)
+
+    with jax.named_scope("second_half"):
+        x1_1 = w_first(1)
+        w_second_dot(1)
+        y1_0 = w1_x(0, x1_0)
+
+    with jax.named_scope("gram_x"):
+        arrive(c_gx)
+        gy[y] = (gx[0] + gx[1]) + (gx[2] + gx[3])
+        c_gy = send_all(FAR, y_peer, lambda yt: gy.at[y], lambda k: gy.at[y], s_gy, r_gy)
+
+    with jax.named_scope("w_sums"):
+        y2_1 = w_second(1)
+        x2_0 = w2_y(0, y2_0)
+        y1_1 = w1_x(1, x1_1)
+
+    with jax.named_scope("gram_y"):
+        arrive(c_gy)
+        gram_all[mine16, :] = ((gy[0] + gy[1]) + (gy[2] + gy[3])) + ((gy[4] + gy[5]) + (gy[6] + gy[7]))
+        c_gz, fs = gather_z(gram_all, s_gz, r_gz, s_gc, r_gc)
+
+    with jax.named_scope("w_gathers"):
+        y1g_0 = w1_y(0, y1_0)
+        x2g_0 = w2_x(0, x2_0)
+        x2_1 = w2_y(1, y2_1)
+        y1g_1 = w1_y(1, y1_1)
+        y2g_1 = w2_x_gather(1, w2_x(1, x2_1))
+
+    with jax.named_scope("gram_z"):
+        gather_core(gram_all, c_gz, fs, s_gc, r_gc)
+        y2g_0 = w2_x_gather(0, x2g_0)
         for c in fs:
             c.wait_recv()
         a[:, :R] = gram_all[...]
-        factor(0, 2)
-
-    with jax.named_scope("w1_y_gather"):
-        for c in c_y1g.values():
-            c.wait_recv()
-        w1x = wf.at[rows8(x * FIRST, FIRST), :]
-        c_x1g = send_all(FAR_X, x_peer, lambda xt: w1x, lambda k: w1x, s_x1g, r_x1g)
-
+
+    with jax.named_scope("factor_first"):
+        x1g_0 = w1_y_gather(0, y1g_0)
+        factor(0, 1)
+    with jax.named_scope("w_last_gathers"):
+        x1g_1 = w1_y_gather(1, y1g_1)
     with jax.named_scope("factor_rest"):
-        factor(2, R // PANEL)
+        factor(1, R // PANEL)
 
     with jax.named_scope("ortho"):
-        ortho_ref[...] = dot3(power[...], a[:, R:], ((1,), (1,)))
+        ortho_ref[...] = dot3(jnp.concatenate([power[0], power[1]], axis=1), a[:, R:], ((1,), (1,)))
     with jax.named_scope("right"):
-        for c in c_x1g.values():
-            c.wait_recv()
-        right_ref[:CUT] = dot3(wf[:CUT], a[:, R:], ((1,), (1,)))
-        for c in c_y2g.values():
-            c.wait_recv()
-        right_ref[CUT:] = dot3(wf[CUT:], a[:, R:], ((1,), (1,)))
+        arrive(x1g_0)
+        arrive(x1g_1)
+        right_ref[: CUT[0]] = dot3(jnp.concatenate([wf[0, : CUT[0]], wf[1, : CUT[0]]], axis=1), a[:, R:], ((1,), (1,)))
+        arrive(y2g_0)
+        arrive(y2g_1)
+        right_ref[CUT[0] :] = dot3(jnp.concatenate([wf[0, CUT[0] :], wf[1, CUT[0] :]], axis=1), a[:, R:], ((1,), (1,)))
     with jax.named_scope("squares"):
         rt = right_ref[...]
         sums = jnp.sum((rt * rt).reshape(COLS // 8, 8, R), axis=0)
@@ -363,8 +425,8 @@
     v = lambda *s: pltpu.VMEM(s, F32)
     d = pltpu.SemaphoreType.DMA
     sems = []
-    for n in (0, 7, 7, 8, 3, 7, 7, 8, 3, 7, 7, 3, 3, 7, 3, 3, 7, 15):
-        sems += [d(()) if n == 0 else d((n,))] * 2
+    for n in (2, (2, 7), (2, 7), (2, 8), 3, 7, 7, 8, (2, 3), (2, 7), (2, 7), (2, 3), (2, 3), (2, 7), (2, 3), (2, 3), (2, 7), 15):
+        sems += [d(n if isinstance(n, tuple) else (n,))] * 2
     out = jax.ShapeDtypeStruct
     vmem = pl.BlockSpec(memory_space=pltpu.VMEM)
     kept = pl.pallas_call(
@@ -374,10 +436,10 @@
         out_specs=vmem,
         scratch_shapes=[
             v(COLS, ROWS), pltpu.VMEM((COLS, ROWS), BF16), v(COLS, R),
-            v(COLS, ROWS), v(ROWS, R), v(128, R), v(128, R), v(7, 16, R), v(ROWS, R),
+            v(COLS, ROWS), v(2, ROWS, 128), v(2, 128, 128), v(2, 128, 128), v(2, 7, 16, 128), v(2, ROWS, 128),
             v(R, R), v(NX, 16, R), v(NY, 16, R), v(R, R),
-            v(COLS, R), v(3, FIRST, R), v(FIRST, R), v(7, SMALL, R), v(7, SECOND, R), v(SECOND, R),
-            v(3, 8, R), v(NX, 8, R), v(COLS, R),
+            v(2, COLS, 128), v(2, 3, FIRST[1], 128), v(2, FIRST[1], 128), v(2, 7, SMALL[1], 128),
+            v(2, 7, SECOND[0], 128), v(2, SECOND[0], 128), v(2, 3, 8, 128), v(2, NX, 8, 128), v(2, COLS, 128),
             v(R, 2 * R), v(2 * NZ, 1, R),
             *sems, d((3,)),
         ],

time: 70.8 us -> 69.5 us (0.982)
  Pallas kernels: 70 us -> 68.7 us
    pallas_call x1, Pallas kernels: 68.6 us -> 67.4 us  [shards(): pl.pallas_call(kernel, out_shape=out((2 * COLS + ROWS + 8, R), F32), in_s...]
where the time goes in v5:
time: 69.5 us; the launch traced here: 69.4 us
  Pallas kernels  68.7 us (99%)
    pallas_call x1, Pallas kernels, shards(): pl.pallas_call(kernel, out_shape=out((2 * COLS + ROWS + 8, R), F32), in_s...  67.4 us

profile of v5, /device:TPU:1, one launch (start us, length us, event | category | flops | bytes accessed | tf_op | source)
XLA Modules:
  0.0 69.4 jit_solution(852718478464395739)
XLA Ops:
  0.6 67.4 %shard_map.58.kept = f32[1928,256]{1,0:T(8,128)S(1)} custom-call(f32[832,256]{1,0:T(8,128)} %bitcast.4, bf16[832,256]{1,0:T(8,128)(2,1)} %bitcast.5, f32[832,256]{1,0:T(8,128)} %basis_hbm.1), custom_call_target="tpu_custom_call" | custom-call | tf_op jit(solution)/shard_map/pallas_call | solution.py:432
  68.0 1.3 %shard_map.59 = (f32[832,256]{1,0:T(8,128)}, f32[832,256]{1,0:T(8,128)}, bf16[832,256]{1,0:T(8,128)(2,1)}) custom-call(f32[1928,256]{1,0:T(8,128)S(1)} %shard_map.58.kept), custom_call_target="tpu_custom_call" | custom-call | tf_op jit(solution)/shard_map/pallas_call | solution.py:450

commit v6 on v5

--- a/solution.py
+++ b/solution.py
@@ -47,7 +47,7 @@
     return one(ah, bh) + (one(ah, bl) + one(al, bh))
 
 
-def factor_panel(k, a):
+def factor_panel(k, a, last=False):
     off = pl.multiple_of(k * PANEL, PANEL)
     base = pl.multiple_of(off // 128 * 128, 128)
     tiles = PANEL // 8
@@ -87,6 +87,8 @@
             t[b][q] = t[b][q] * scale
     r = jnp.concatenate([jnp.concatenate(t[i][1:], axis=1) for i in range(tiles)], axis=0)
     a[pl.ds(off, PANEL), R:] = r[:, R:]
+    if last:
+        return
     hi = r.astype(BF16).astype(F32)
     mi = (r - hi).astype(BF16).astype(F32)
     lo = r - hi - mi
@@ -115,10 +117,13 @@
 ):
     nm_ref, right_ref, ortho_ref, norms_ref = (out_ref.at[pl.ds(at, n), :] for at, n in KEPT)
     loads = [
-        pltpu.make_async_copy(src, dst, s_in.at[i])
-        for i, (src, dst) in enumerate(((mom_hbm, mom_ref), (grad_hbm, grad_ref), (basis_hbm, basis_ref)))
+        [
+            pltpu.make_async_copy(src.at[pl.ds(at, COLS // 2), :], dst.at[pl.ds(at, COLS // 2), :], s_in.at[i, q])
+            for i, (src, dst) in enumerate(((mom_hbm, mom_ref), (grad_hbm, grad_ref), (basis_hbm, basis_ref)))
+        ]
+        for q, at in enumerate((0, COLS // 2))
     ]
-    for load in loads:
+    for load in loads[0] + loads[1]:
         load.start()
     row = lax.axis_index("row")
     col = lax.axis_index("col")
@@ -171,9 +176,10 @@
     theirs128 = rows8((1 - core) * 128, 128)
     mine16 = rows8(core * 128 + z * 16, 16)
 
-    def part_power(half_core):
+    def part_power(half_core, q):
         lanes = pl.ds(pl.multiple_of(half_core * 128, 128), 128)
-        return dot(buf[:, lanes], basis_ref[...], ((0,), (0,)))
+        some = pl.ds(q * (COLS // 2), COLS // 2)
+        return dot(buf[some, lanes], basis_ref[some, :], ((0,), (0,)))
 
     def send_all(order, peer, src, dst, ss, rr):
         out = {}
@@ -187,15 +193,21 @@
             c.wait_recv()
 
     with jax.named_scope("partial_power"):
-        for load in loads:
-            load.wait()
-        buf[...] = mom_ref[...] + grad_ref[...].astype(F32)
-        theirs = part_power(1 - core)
+        theirs, mine = [], []
+        for q in range(2):
+            for load in loads[q]:
+                load.wait()
+            some = pl.ds(q * (COLS // 2), COLS // 2)
+            buf[some, :] = mom_ref[some, :] + grad_ref[some, :].astype(F32)
+            theirs.append(part_power(1 - core, q))
+            if q == 0:
+                mine.append(part_power(core, q))
+        theirs = theirs[0] + theirs[1]
         for h in HALVES:
             part[h, theirs128, :] = theirs[:, 128 * h : 128 * h + 128]
         pl.semaphore_wait(barrier, len(peers))
         c_core = [send(part.at[h, theirs128, :], core_in.at[h], s_core.at[h], r_core.at[h], sibling) for h in HALVES]
-        mine = part_power(core)
+        mine = mine[0] + part_power(core, 1)
 
     c_z = [None, None]
     with jax.named_scope("power_core"):
@@ -367,10 +379,9 @@
     with jax.named_scope("w_last_gathers"):
         x1g_1 = w1_y_gather(1, y1g_1)
     with jax.named_scope("factor_rest"):
-        factor(1, R // PANEL)
-
-    with jax.named_scope("ortho"):
-        ortho_ref[...] = dot3(jnp.concatenate([power[0], power[1]], axis=1), a[:, R:], ((1,), (1,)))
+        factor(1, R // PANEL - 1)
+        factor_panel(jnp.int32(R // PANEL - 1), a, last=True)
+
     with jax.named_scope("right"):
         arrive(x1g_0)
         arrive(x1g_1)
@@ -387,6 +398,8 @@
             for k in (8, 7, 9, 6, 10, 5, 11, 4, 12, 3, 13, 2, 14, 1, 15)
         ]
 
+    with jax.named_scope("ortho"):
+        ortho_ref[...] = dot3(jnp.concatenate([power[0], power[1]], axis=1), a[:, R:], ((1,), (1,)))
     with jax.named_scope("momentum"):
         nm_ref[...] = buf[...] - (1.0 - KEEP_RATE) * dot3(right_ref[...], ortho_ref[...], ((1,), (1,)))
 
@@ -441,7 +454,7 @@
             v(2, COLS, 128), v(2, 3, FIRST[1], 128), v(2, FIRST[1], 128), v(2, 7, SMALL[1], 128),
             v(2, 7, SECOND[0], 128), v(2, SECOND[0], 128), v(2, 3, 8, 128), v(2, NX, 8, 128), v(2, COLS, 128),
             v(R, 2 * R), v(2 * NZ, 1, R),
-            *sems, d((3,)),
+            *sems, d((3, 2)),
         ],
         compiler_params=pltpu.CompilerParams(
             collective_id=0, has_side_effects=True, vmem_limit_bytes=40 << 20

time: 69.5 us -> 69 us (level)
  no operation moved by 1% of the time
where the time goes in v6:
time: 69 us; the launch traced here: 68.9 us
  Pallas kernels  68.2 us (99%)
    pallas_call x1, Pallas kernels, shards(): pl.pallas_call(kernel, out_shape=out((2 * COLS + ROWS + 8, R), F32), in_s...  66.9 us

profile of v6, /device:TPU:1, one launch (start us, length us, event | category | flops | bytes accessed | tf_op | source)
XLA Modules:
  0.0 68.9 jit_solution(5796350399990006986)
XLA Ops:
  0.6 66.9 %shard_map.58.kept = f32[1928,256]{1,0:T(8,128)S(1)} custom-call(f32[832,256]{1,0:T(8,128)} %bitcast.4, bf16[832,256]{1,0:T(8,128)(2,1)} %bitcast.5, f32[832,256]{1,0:T(8,128)} %basis_hbm.1), custom_call_target="tpu_custom_call" | custom-call | tf_op jit(solution)/shard_map/pallas_call | solution.py:445
  67.5 1.3 %shard_map.59 = (f32[832,256]{1,0:T(8,128)}, f32[832,256]{1,0:T(8,128)}, bf16[832,256]{1,0:T(8,128)(2,1)}) custom-call(f32[1928,256]{1,0:T(8,128)S(1)} %shard_map.58.kept), custom_call_target="tpu_custom_call" | custom-call | tf_op jit(solution)/shard_map/pallas_call | solution.py:463

commit v7 on v6

--- a/solution.py
+++ b/solution.py
@@ -335,8 +335,8 @@
 
     with jax.named_scope("gram_dot"):
         whole = jnp.concatenate([power[0], power[1]], axis=1)
-        gram[...] = dot(whole, whole, ((0,), (0,)))
-        gx[x] = gram[mine16, :]
+        gram[...] = dot(power[core], whole, ((0,), (0,)))
+        gx[x] = gram[rows8(z * 16, 16), :]
         c_gx = send_all(FAR_X, x_peer, lambda xt: gx.at[x], lambda k: gx.at[x], s_gx, r_gx)
 
     with jax.named_scope("second_half"):
@@ -450,7 +450,7 @@
         scratch_shapes=[
             v(COLS, ROWS), pltpu.VMEM((COLS, ROWS), BF16), v(COLS, R),
             v(COLS, ROWS), v(2, ROWS, 128), v(2, 128, 128), v(2, 128, 128), v(2, 7, 16, 128), v(2, ROWS, 128),
-            v(R, R), v(NX, 16, R), v(NY, 16, R), v(R, R),
+            v(128, R), v(NX, 16, R), v(NY, 16, R), v(R, R),
             v(2, COLS, 128), v(2, 3, FIRST[1], 128), v(2, FIRST[1], 128), v(2, 7, SMALL[1], 128),
             v(2, 7, SECOND[0], 128), v(2, SECOND[0], 128), v(2, 3, 8, 128), v(2, NX, 8, 128), v(2, COLS, 128),
             v(R, 2 * R), v(2 * NZ, 1, R),

time: 69 us -> 68.1 us (0.987)
  Pallas kernels: 68.2 us -> 67.3 us
    pallas_call x1, Pallas kernels: 66.9 us -> 65.9 us  [shards(): pl.pallas_call(kernel, out_shape=out((2 * COLS + ROWS + 8, R), F32), in_s...]
where the time goes in v7:
time: 68.1 us; the launch traced here: 67.9 us
  Pallas kernels  67.3 us (99%)
    pallas_call x1, Pallas kernels, shards(): pl.pallas_call(kernel, out_shape=out((2 * COLS + ROWS + 8, R), F32), in_s...  65.9 us

profile of v7, /device:TPU:1, one launch (start us, length us, event | category | flops | bytes accessed | tf_op | source)
XLA Modules:
  0.0 67.9 jit_solution(8919290458764035275)
XLA Ops:
  0.6 65.9 %shard_map.58.kept = f32[1928,256]{1,0:T(8,128)S(1)} custom-call(f32[832,256]{1,0:T(8,128)} %bitcast.4, bf16[832,256]{1,0:T(8,128)(2,1)} %bitcast.5, f32[832,256]{1,0:T(8,128)} %basis_hbm.1), custom_call_target="tpu_custom_call" | custom-call | tf_op jit(solution)/shard_map/pallas_call | solution.py:445
  66.6 1.3 %shard_map.59 = (f32[832,256]{1,0:T(8,128)}, f32[832,256]{1,0:T(8,128)}, bf16[832,256]{1,0:T(8,128)(2,1)}) custom-call(f32[1928,256]{1,0:T(8,128)S(1)} %shard_map.58.kept), custom_call_target="tpu_custom_call" | custom-call | tf_op jit(solution)/shard_map/pallas_call | solution.py:463
